TPU v7x, 128 devices: a whole 4x4x4 slice. The times are simulated.
128 devices in a mesh: dp: 4 (over x), expert: 8 (over z, core), mp: 4 (over y).
Axes of the slice: x: 4, y: 4, z: 4, core: 2. Of those that a mesh axis runs over, the one named last changes fastest.
Arguments:
- tokens: bfloat16 [8192, 2048], P(('dp', 'expert')), may hold values from -6 to 6
- attn_norm: float32 [2048], replicated, may hold values from 0.5 to 1.5
- qkv_weights: bfloat16 [3, 2048, 2048], P(None, ('dp', 'expert'), 'mp'), may hold values from -0.125 to 0.125
- out_weight: bfloat16 [2048, 2048], P(('dp', 'expert'), 'mp'), may hold values from -0.5 to 0.5
- q_gain: float32 [2048], P('mp'), may hold values from 0.1 to 1.9
- k_gain: float32 [2048], P('mp'), may hold values from 0.1 to 1.9
- ffn_norm: float32 [2048], replicated, may hold values from 0.5 to 1.5
- router: bfloat16 [2048, 64], replicated, may hold values from -0.0625 to 0.0625
- expert_weights: bfloat16 [64, 3, 2048, 1024], P(('dp', 'expert'), None, None, 'mp'), may hold values from -6 to 6
- lengths: int32 [32, 4], P(('dp', 'expert')), may hold values from 1 to 192, 256 in all within a row
- expert_ids: int32 [8192, 8], P(('dp', 'expert')), may hold values from 0 to 63, all different within a row; in each aligned block of 256 rows (0 to 255, 256 to 511, ...) at most 48 rows name the same one
- cotangent: bfloat16 [8192, 2048], P(('dp', 'expert')), may hold values from -6 to 6
Outputs:
- out: bfloat16 [8192, 2048], P(('dp', 'expert'))
- input_grad: float32 [8192, 2048], P(('dp', 'expert'))
- grad_attn_norm: float32 [2048], replicated
- grad_qkv: float32 [3, 2048, 2048], P(None, ('dp', 'expert'), 'mp')
- grad_out_weight: float32 [2048, 2048], P(('dp', 'expert'), 'mp')
- grad_q_gain: float32 [2048], P('mp')
- grad_k_gain: float32 [2048], P('mp')
- grad_ffn_norm: float32 [2048], replicated
- grad_router: float32 [2048, 64], replicated
- grad_experts: float32 [64, 2, 2048, 1024], P(('dp', 'expert'), None, None, 'mp')
- grad_down: float32 [64, 2048, 1024], P(('dp', 'expert'), None, 'mp')
Inputs may be any that keep to these rules, and one draw needn't show every extreme that they name: `expert_ids`: each row names 8 different experts. Within each aligned block of 256 rows (one token group) no expert is named by more than 48 rows, and in some block an expert is named by exactly 48. `lengths`: each row sums to 256, and its largest entry is 192.
All inputs are finite; a program needn't handle non-finite values.
Results may differ from a plain program's by a relative error of at most 0.025.
Values may be sent and summed in bfloat16 or wider, within the bound.
A program may use at most 256 MiB of HBM per device.

v0:
```python
import jax
import jax.numpy as jnp
from jax import lax
from jax.sharding import PartitionSpec as P

HEADS = 16
HEAD = 128


EPSILON = 1e-05


def norm_stats(values):
    scale_inv = lax.rsqrt(jnp.mean(values * values, axis=-1, keepdims=True) + EPSILON)
    return (values * scale_inv, scale_inv)


def norm_back(d_hat, hat, scale_inv):
    return scale_inv * (d_hat - hat * jnp.mean(d_hat * hat, axis=-1, keepdims=True))


def rope_tables(position):
    half = HEAD // 2
    freqs = 10000.0 ** (-jnp.arange(half, dtype=jnp.float32) / half)
    angles = position.astype(jnp.float32)[:, None] * freqs[None, :]
    return (jnp.cos(angles)[:, None, :], jnp.sin(angles)[:, None, :])


def rotate(values, cosine, sine):
    half = HEAD // 2
    first = values[..., :half]
    second = values[..., half:]
    return jnp.concatenate(
        [first * cosine - second * sine, second * cosine + first * sine], axis=-1
    )


def unrotate(grads, cosine, sine):
    half = HEAD // 2
    first = grads[..., :half]
    second = grads[..., half:]
    return jnp.concatenate(
        [first * cosine + second * sine, second * cosine - first * sine], axis=-1
    )


def layout(lengths_row, tok_rows):
    index = jnp.arange(tok_rows, dtype=jnp.int32)
    ends = jnp.cumsum(lengths_row, dtype=jnp.int32)
    starts = ends - lengths_row
    segment = jnp.sum((index[:, None] >= ends[None, :]).astype(jnp.int32), axis=1, dtype=jnp.int32)
    chosen = segment[:, None] == jnp.arange(lengths_row.shape[0], dtype=jnp.int32)[None, :]
    position = index - jnp.sum(jnp.where(chosen, starts[None, :], 0), axis=1, dtype=jnp.int32)
    allowed = (segment[:, None] == segment[None, :]) & (index[None, :] <= index[:, None])
    return (position, allowed)


def body(
    tokens,
    attn_norm,
    qkv_weights,
    out_weight,
    q_gain,
    k_gain,
    ffn_norm,
    router,
    expert_weights,
    lengths,
    expert_ids,
    cotangent,
):
    tok_rows, width = tokens.shape
    choose = expert_ids.shape[1]
    groups = lax.axis_size(("dp", "expert"))
    model_split = lax.axis_size("mp")
    local_experts = expert_weights.shape[0]
    expert_count = groups * local_experts
    capacity = (
        (tok_rows * choose * 3 // (expert_count * 2) + model_split - 1) // model_split * model_split
    )
    quarter = capacity // model_split
    head_cols = q_gain.shape[0]
    local_heads = head_cols // HEAD
    full_cols = HEADS * HEAD
    score_scale = HEAD ** (-0.5)
    bf16 = jnp.bfloat16
    f32 = jnp.float32
    hidden = tokens.astype(f32)
    blocks = jnp.concatenate([qkv_weights, out_weight[None]], axis=0)
    gathered = lax.all_gather(blocks, ("dp", "expert"), axis=1, tiled=True)
    proj_weights = gathered[:3]
    out_full = gathered[3]
    attn_hat, attn_inv = norm_stats(hidden)
    normed_b = (attn_hat * attn_norm).astype(bf16)
    projected = jnp.einsum("td,jdc->jtc", normed_b, proj_weights, preferred_element_type=f32)
    query_raw = projected[0]
    key_raw = projected[1]
    square_sums = lax.psum(
        (
            jnp.sum(query_raw * query_raw, axis=-1, keepdims=True),
            jnp.sum(key_raw * key_raw, axis=-1, keepdims=True),
        ),
        "mp",
    )
    query_inv = lax.rsqrt(square_sums[0] / full_cols + EPSILON)
    key_inv = lax.rsqrt(square_sums[1] / full_cols + EPSILON)
    query_hat = query_raw * query_inv
    key_hat = key_raw * key_inv
    position, allowed = layout(lengths[0], tok_rows)
    cosine, sine = rope_tables(position)
    query_b = rotate(
        (query_hat * q_gain).reshape(tok_rows, local_heads, HEAD), cosine, sine
    ).astype(bf16)
    key_b = rotate((key_hat * k_gain).reshape(tok_rows, local_heads, HEAD), cosine, sine).astype(
        bf16
    )
    value_b = projected[2].astype(bf16).reshape(tok_rows, local_heads, HEAD)
    raw_scores = (
        jnp.einsum("qhc,khc->hqk", query_b, key_b, preferred_element_type=f32) * score_scale
    )
    masked = jnp.where(allowed[None], raw_scores, -1e30)
    row_top = jnp.max(masked, axis=-1, keepdims=True)
    log_total = row_top + jnp.log(jnp.sum(jnp.exp(masked - row_top), axis=-1, keepdims=True))
    probs_b = jnp.exp(masked - log_total).astype(bf16)
    mixed_b = jnp.einsum("hqk,khc->qhc", probs_b, value_b, preferred_element_type=f32).astype(bf16)
    mixed_b = mixed_b.reshape(tok_rows, head_cols)
    attn_part = jnp.einsum("tc,dc->td", mixed_b, out_full, preferred_element_type=f32)
    resid = hidden + lax.psum(attn_part, "mp")
    ffn_hat, ffn_inv = norm_stats(resid)
    moe_in = (ffn_hat * ffn_norm).astype(bf16)
    logits = jnp.dot(moe_in, router, preferred_element_type=f32)
    weights = jax.nn.softmax(logits, axis=-1)
    picks = (
        expert_ids[:, :, None] == jnp.arange(expert_count, dtype=jnp.int32)[None, None, :]
    ).astype(f32)
    gates = jnp.sum(weights[:, None, :] * picks, axis=-1)
    flat = expert_ids.reshape(-1)
    onehot = (flat[:, None] == jnp.arange(expert_count, dtype=jnp.int32)[None, :]).astype(jnp.int32)
    slot = jnp.sum(
        (jnp.cumsum(onehot, axis=0, dtype=jnp.int32) - onehot) * onehot, axis=1, dtype=jnp.int32
    )
    dest = flat * capacity + slot
    send = (
        jnp.zeros((expert_count * capacity, width), bf16)
        .at[dest]
        .set(jnp.repeat(moe_in, choose, axis=0))
    )
    send = send.reshape(groups, local_experts, capacity, width)
    received = lax.all_to_all(send, ("dp", "expert"), split_axis=0, concat_axis=0, tiled=True)
    gate_pre = jnp.einsum(
        "sjcd,jdf->sjcf", received, expert_weights[:, 0], preferred_element_type=f32
    )
    up_pre = jnp.einsum(
        "sjcd,jdf->sjcf", received, expert_weights[:, 1], preferred_element_type=f32
    )
    sigmoid_gate = jax.nn.sigmoid(gate_pre)
    silu_gate = gate_pre * sigmoid_gate
    inner_b = (silu_gate * up_pre).astype(bf16)
    expert_part = jnp.einsum(
        "sjcf,jdf->sjcd", inner_b, expert_weights[:, 2], preferred_element_type=f32
    )
    expert_quarter = lax.psum_scatter(expert_part, "mp", scatter_dimension=2, tiled=True).astype(
        bf16
    )
    returned = lax.all_to_all(
        expert_quarter, ("dp", "expert"), split_axis=0, concat_axis=0, tiled=True
    ).reshape(expert_count * quarter, width)
    low_slot = lax.axis_index("mp") * quarter
    mine = (slot >= low_slot) & (slot < low_slot + quarter)
    local_index = flat * quarter + jnp.clip(slot - low_slot, 0, quarter - 1)
    picked = jnp.where(mine[:, None], returned[local_index].astype(f32), 0.0).reshape(
        tok_rows, choose, width
    )
    moe_part = jnp.sum(gates[:, :, None] * picked, axis=1)
    d_out = cotangent.astype(f32)
    d_gate_part = jnp.sum(picked * d_out[:, None, :], axis=2)
    d_rows_out = (
        (gates[:, :, None] * d_out[:, None, :]).reshape(tok_rows * choose, width).astype(bf16)
    )
    grad_send = jnp.zeros((expert_count * capacity, width), bf16).at[dest].set(d_rows_out)
    grad_send = grad_send.reshape(groups, local_experts, capacity, width)
    grad_recv = lax.all_to_all(grad_send, ("dp", "expert"), split_axis=0, concat_axis=0, tiled=True)
    d_inner = jnp.einsum(
        "sjcd,jdf->sjcf", grad_recv, expert_weights[:, 2], preferred_element_type=f32
    )
    grad_down = jnp.einsum("sjcd,sjcf->jdf", grad_recv, inner_b, preferred_element_type=f32)
    d_gate_b = (d_inner * up_pre * sigmoid_gate * (1.0 + gate_pre * (1.0 - sigmoid_gate))).astype(
        bf16
    )
    d_up_b = (d_inner * silu_gate).astype(bf16)
    grad_gate = jnp.einsum("sjcd,sjcf->jdf", received, d_gate_b, preferred_element_type=f32)
    grad_up = jnp.einsum("sjcd,sjcf->jdf", received, d_up_b, preferred_element_type=f32)
    d_rows = jnp.einsum(
        "sjcf,jdf->sjcd", d_gate_b, expert_weights[:, 0], preferred_element_type=f32
    )
    d_rows = d_rows + jnp.einsum(
        "sjcf,jdf->sjcd", d_up_b, expert_weights[:, 1], preferred_element_type=f32
    )
    grad_experts = jnp.stack([grad_gate, grad_up], axis=1)
    back = lax.all_to_all(
        d_rows, ("dp", "expert"), split_axis=0, concat_axis=0, tiled=True
    ).reshape(expert_count * capacity, width)
    back_rows = back[dest]
    dm_part = jnp.sum(back_rows.reshape(tok_rows, choose, width), axis=1)
    moe_total, dm_experts, d_gates = (
        lax.psum(moe_part.astype(jnp.bfloat16), "mp").astype(jnp.float32),
        lax.psum(dm_part.astype(jnp.bfloat16), "mp").astype(jnp.float32),
        lax.psum(d_gate_part.astype(jnp.bfloat16), "mp").astype(jnp.float32),
    )
    output = resid + moe_total
    d_weights = jnp.sum(d_gates[:, :, None] * picks, axis=1)
    d_logits_b = (
        weights * (d_weights - jnp.sum(weights * d_weights, axis=-1, keepdims=True))
    ).astype(bf16)
    grad_router = jnp.einsum("td,te->de", moe_in, d_logits_b, preferred_element_type=f32)
    d_moe_in = dm_experts + jnp.einsum("te,de->td", d_logits_b, router, preferred_element_type=f32)
    grad_ffn = jnp.sum(d_moe_in * ffn_hat, axis=0)
    d_resid = d_out + norm_back(d_moe_in * ffn_norm, ffn_hat, ffn_inv)
    d_resid_b = d_resid.astype(bf16)
    grad_out = jnp.einsum("td,tc->dc", d_resid_b, mixed_b, preferred_element_type=f32)
    d_mixed_b = jnp.einsum("td,dc->tc", d_resid_b, out_full, preferred_element_type=f32).astype(
        bf16
    )
    d_mixed_b = d_mixed_b.reshape(tok_rows, local_heads, HEAD)
    again = jnp.einsum("qhc,khc->hqk", query_b, key_b, preferred_element_type=f32) * score_scale
    probs = jnp.where(
        allowed[None], jnp.exp(jnp.where(allowed[None], again, -1e30) - log_total), 0.0
    )
    probs_again_b = probs.astype(bf16)
    d_value = jnp.einsum("hqk,qhc->khc", probs_again_b, d_mixed_b, preferred_element_type=f32)
    d_probs = jnp.einsum("qhc,khc->hqk", d_mixed_b, value_b, preferred_element_type=f32)
    d_scores_b = (probs * (d_probs - jnp.sum(probs * d_probs, axis=-1, keepdims=True))).astype(bf16)
    d_query_rot = (
        jnp.einsum("hqk,khc->qhc", d_scores_b, key_b, preferred_element_type=f32) * score_scale
    )
    d_key_rot = (
        jnp.einsum("hqk,qhc->khc", d_scores_b, query_b, preferred_element_type=f32) * score_scale
    )
    d_query_n = unrotate(d_query_rot, cosine, sine).reshape(tok_rows, head_cols)
    d_key_n = unrotate(d_key_rot, cosine, sine).reshape(tok_rows, head_cols)
    grad_q_gain = jnp.sum(d_query_n * query_hat, axis=0)
    grad_k_gain = jnp.sum(d_key_n * key_hat, axis=0)
    query_scaled = d_query_n * q_gain
    key_scaled = d_key_n * k_gain
    mean_terms = lax.psum(
        (
            jnp.sum(query_scaled * query_hat, axis=-1, keepdims=True),
            jnp.sum(key_scaled * key_hat, axis=-1, keepdims=True),
        ),
        "mp",
    )
    d_query_b = (query_inv * (query_scaled - query_hat * (mean_terms[0] / full_cols))).astype(bf16)
    d_key_b = (key_inv * (key_scaled - key_hat * (mean_terms[1] / full_cols))).astype(bf16)
    d_value_b = d_value.astype(bf16).reshape(tok_rows, head_cols)
    d_proj = jnp.stack([d_query_b, d_key_b, d_value_b], axis=0)
    grad_proj = jnp.einsum("td,jtc->jdc", normed_b, d_proj, preferred_element_type=f32)
    d_normed_part = jnp.einsum("jtc,jdc->td", d_proj, proj_weights, preferred_element_type=f32)
    d_normed = lax.psum(d_normed_part.astype(jnp.bfloat16), "mp").astype(jnp.float32)
    grad_attn = jnp.sum(d_normed * attn_hat, axis=0)
    input_grad = d_resid + norm_back(d_normed * attn_norm, attn_hat, attn_inv)
    block_grads = jnp.concatenate([grad_proj, grad_out[None]], axis=0)
    scattered = lax.psum_scatter(
        block_grads.astype(jnp.bfloat16), ("dp", "expert"), scatter_dimension=1, tiled=True
    ).astype(jnp.float32)
    small = (
        lax.psum(grad_attn.astype(jnp.bfloat16), ("dp", "expert")).astype(jnp.float32),
        lax.psum(grad_ffn.astype(jnp.bfloat16), ("dp", "expert")).astype(jnp.float32),
        lax.psum(grad_q_gain.astype(jnp.bfloat16), ("dp", "expert")).astype(jnp.float32),
        lax.psum(grad_k_gain.astype(jnp.bfloat16), ("dp", "expert")).astype(jnp.float32),
        lax.psum(grad_router.astype(jnp.bfloat16), ("dp", "expert")).astype(jnp.float32),
    )
    return (
        output.astype(bf16),
        input_grad,
        small[0],
        scattered[:3],
        scattered[3],
        small[2],
        small[3],
        small[1],
        small[4],
        grad_experts,
        grad_down,
    )


def solution(mesh):
    placed = (
        P(("dp", "expert"), None),
        P(),
        P(None, ("dp", "expert"), "mp"),
        P(("dp", "expert"), "mp"),
        P("mp"),
        P("mp"),
        P(),
        P(),
        P(("dp", "expert"), None, None, "mp"),
        P(("dp", "expert"), None),
        P(("dp", "expert"), None),
        P(("dp", "expert"), None),
    )
    return jax.shard_map(
        body,
        mesh=mesh,
        in_specs=placed,
        out_specs=(
            P(("dp", "expert"), None),
            P(("dp", "expert"), None),
            P(),
            P(None, ("dp", "expert"), "mp"),
            P(("dp", "expert"), "mp"),
            P("mp"),
            P("mp"),
            P(),
            P(),
            P(("dp", "expert"), None, None, "mp"),
            P(("dp", "expert"), None, "mp"),
        ),
        check_vma=False,
    )
```

profile of v0, /device:TPU:0, one launch (start us, length us, event | category | flops | bytes accessed | tf_op | source)
XLA Modules:
  0.0 1680.4 jit_solution(3385083148734851425)
XLA Ops:
  14.3 52.1 %all-gather.2.cloned.1.call-done = bf16[4,2048,512]{2,0,1:T(4,128)(2,1)} async-done(((bf16[4,64,512]{2,0,1:T(4,128)(2,1)}), bf16[4,2048,512]{2,0,1:T(4,128)(2,1)}) %all-gather.2.cloned.1.call-update) | async-done | bytes 8388624 | tf_op jit(solution)/shard_map/all_gather | solution.py:90
  66.4 13.2 copy.290
  110.8 18.1 %reduce-window.11 = s32[64,16,128]{2,1,0:T(8,128)S(1)} reduce-window(s32[64,16,128]{2,1,0:T(8,128)S(1)} %fusion.80, s32[]{:T(128)} %constant.20.clone.1), window={size=1x1x128 pad=0_0x0_0x127_0}, to_apply=%region_15.16 | reduce-window | flops 16646144 | bytes 1048580 | tf_op jit(solution)/shard_map/reduce-window.1
  130.3 35.5 %all-reduce.11.cloned.1.call-done = f32[256,2048]{1,0:T(8,128)} async-done(((f32[256,2048]{1,0:T(8,128)}), f32[256,2048]{1,0:T(8,128)}) %all-reduce.11.cloned.1.call-update) | async-done | bytes 2097168 | tf_op jit(solution)/shard_map/psum | solution.py:128
  169.3 19.1 %scatter_custom_fusion = bf16[3072,2048]{1,0:T(8,128)(2,1)} fusion(s32[2048]{0:T(1024)S(1)} %bitcast.250, bf16[]{:T(256)} %constant.52.clone.1, bf16[256,2048]{1,0:T(8,128)(2,1)S(1)} %multiply_convert_fusion), kind=kCustom, calls=%fused_computation.25 | custom fusion | bytes 13631490 | tf_op jit(solution)/shard_map/scatter | solution.py:146
  188.4 148.2 %all_to_all.20 = bf16[32,2,48,2048]{3,2,1,0:T(8,128)(2,1)} all-to-all(bf16[32,2,48,2048]{3,2,1,0:T(8,128)(2,1)} %bitcast.231), channel_id=1, replica_groups=mesh['dp'=4,'expert'=8,'mp'=4] {'dp','expert'}, dimensions={0} | all-to-all | bytes 25165824 | tf_op jit(solution)/shard_map/all_to_all | solution.py:149
  358.5 12.3 convolution_bitcast_fusion
  370.8 24.9 %copy.244 = f32[32,2,48,2048]{3,0,1,2:T(8,128)} copy(f32[32,2,48,2048]{3,2,0,1:T(8,128)} %convolution_bitcast_fusion) | data formatting | bytes 50331648 | tf_op jit(solution)/shard_map/sjcf,jdf->sjcd/transpose | solution.py:159
  395.7 212.3 %reduce-scatter.2.cloned.1.call-done = f32[32,2,12,2048]{3,0,1,2:T(8,128)} async-done(((f32[32,2,48,2048]{3,0,1,2:T(8,128)}), f32[32,2,12,2048]{3,0,1,2:T(8,128)}) %reduce-scatter.2.cloned.1.call-update) | async-done | bytes 6291472 | tf_op jit(solution)/shard_map/reduce_scatter | solution.py:162
  626.5 37.2 %all-to-all-done.1 = bf16[32,2,12,2048]{3,1,2,0:T(2,128)(2,1)} async-done(((bf16[32,2,12,2048]{3,1,2,0:T(2,128)(2,1)}), bf16[32,2,12,2048]{3,1,2,0:T(2,128)(2,1)}, u32[]{:S(2)}, u32[]{:S(2)}) %all-to-all-start.1) | async-done | bytes 3145760 | tf_op jit(solution)/shard_map/all_to_all | solution.py:165
  700.3 20.1 %scatter_custom_fusion.1 = bf16[3072,2048]{1,0:T(8,128)(2,1)} fusion(s32[2048]{0:T(1024)S(1)} %bitcast.251, f32[256,2048]{1,0:T(8,128)S(1)} %copy-done.9, f32[2048]{0:T(1024)S(1)} %mul.560, bf16[]{:T(256)} %constant.52.clone.1), kind=kCustom, calls=%fused_computation.22 | custom fusion | flops 8388608 | bytes 14688258 | tf_op jit(solution)/shard_map/scatter | solution.py:180
  720.4 145.9 %all_to_all.21 = bf16[32,2,48,2048]{3,2,1,0:T(8,128)(2,1)} all-to-all(bf16[32,2,48,2048]{3,2,1,0:T(8,128)(2,1)} %bitcast.230), channel_id=1, replica_groups=mesh['dp'=4,'expert'=8,'mp'=4] {'dp','expert'}, dimensions={0} | all-to-all | bytes 25165824 | tf_op jit(solution)/shard_map/all_to_all | solution.py:182
  866.3 11.6 fusion.23
  877.9 12.8 fusion.42
  890.7 17.0 %add_bitcast_fusion = f32[32,2,48,2048]{3,2,0,1:T(8,128)} fusion(f32[2,32,48,2048]{3,2,1,0:T(8,128)} %fusion.42, bf16[32,2,48,256]{3,2,0,1:T(8,128)(2,1)S(1)} %get-tuple-element.105, bf16[2,3,2048,256]{3,2,1,0:T(8,128)(2,1)} %param.20), kind=kOutput, calls=%fused_computation.6 | convolution fusion | flops 3227516928 | bytes 54001664 | tf_op jit(solution)/shard_map/sjcf,jdf->sjcd/dot_general | solution.py:196
  907.7 17.4 %copy.250 = f32[32,2,48,2048]{3,2,1,0:T(8,128)} copy(f32[32,2,48,2048]{3,2,0,1:T(8,128)} %add_bitcast_fusion) | data formatting | bytes 50331648 | tf_op jit(solution)/shard_map/add | solution.py:196
  932.2 361.4 %all-to-all-done.3 = f32[32,2,48,2048]{3,2,1,0:T(8,128)} async-done(((f32[32,2,48,2048]{3,2,1,0:T(8,128)}), f32[32,2,48,2048]{3,2,1,0:T(8,128)}, u32[]{:S(2)}, u32[]{:S(2)}) %all-to-all-start.3) | async-done | bytes 25165856 | tf_op jit(solution)/shard_map/all_to_all | solution.py:200
  1293.6 24.7 %gather_fusion.1 = f32[2048,2048]{1,0:T(8,128)} fusion(f32[3072,2048]{1,0:T(8,128)} %bitcast.47, s32[2048]{0:T(1024)S(1)} %broadcast_clamp_fusion), kind=kCustom, calls=%fused_computation.1 | custom fusion | bytes 33562624 | tf_op jit(solution)/shard_map/gather | solution.py:203
  1339.4 80.9 %all-reduce.13.cloned.1.call-done = bf16[256,2048]{1,0:T(8,128)(2,1)} async-done(((bf16[256,2048]{1,0:T(8,128)(2,1)}), bf16[256,2048]{1,0:T(8,128)(2,1)}) %all-reduce.13.cloned.1.call-update) | async-done | bytes 1048592 | tf_op jit(solution)/shard_map/psum | solution.py:207
  1459.6 12.0 convolution_bitcast_fusion.2
  1485.8 15.0 copy.267
  1500.8 12.1 convolution_bitcast_fusion.3
  1520.9 12.0 convolution_bitcast_fusion.1
  1535.0 126.9 %all-reduce.3 = (bf16[2048]{0:T(1024)(128)(2,1)S(1)}, bf16[512]{0:T(512)(128)(2,1)S(1)}, bf16[512]{0:T(512)(128)(2,1)S(1)}, bf16[2048]{0:T(1024)(128)(2,1)S(1)}) all-reduce(bf16[2048]{0:T(1024)(128)(2,1)S(1)} %get-tuple-element.83, ...), channel_id=1, replica_groups=mesh['dp'=4,'expert'=8,'mp'=4] {'dp','expert'}, use_global_device_ids=true, to_apply=%region_38.39 | all-reduce | flops 5120 | bytes 20480 | tf_op jit(solution)/shard_map/psum | solution.py:266
  (277 shorter events, 221.4 us)
Async XLA Ops:
  7.2 618.1 %copy-start = (bf16[2048,64]{0,1:T(8,128)(2,1)S(1)}, bf16[2048,64]{0,1:T(8,128)(2,1)}, u32[]{:S(2)}) copy-start(bf16[2048,64]{0,1:T(8,128)(2,1)} %param.19) | copy-start | bytes 786436
  7.2 59.2 %all-gather.2.cloned.1.call-start = ((), (), s32[]{:S(2)}) async-start(), calls=%async_computation.5 | async-start | bytes 8650752 | tf_op jit(solution)/shard_map/all_gather | solution.py:90
  10.3 155.5 %all-reduce.11.cloned.1.call-start = ((), (), s32[]{:S(2)}) async-start(), calls=%async_computation.6 | async-start | bytes 4194304 | tf_op jit(solution)/shard_map/psum | solution.py:128
  13.6 66.0 %copy-start.66 = (f32[256]{0:T(256)}, f32[256]{0:T(256)S(1)}, u32[]{:S(2)}) copy-start(f32[256]{0:T(256)S(1)} %add_rsqrt_fusion.3) | copy-start | bytes 3076
  13.7 83.7 %copy-start.28 = (pred[256,256]{0,1:T(8,128)(4,1)}, pred[256,256]{0,1:T(8,128)(4,1)S(1)}, u32[]{:S(2)}) copy-start(pred[256,256]{0,1:T(8,128)(4,1)S(1)} %fusion.82) | copy-start | bytes 196612
  14.2 82.6 %copy-start.35 = (f32[256,64]{1,0:T(8,128)}, f32[256,64]{1,0:T(8,128)S(1)}, u32[]{:S(2)}) copy-start(f32[256,64]{1,0:T(8,128)S(1)} %get-tuple-element.127) | copy-start | bytes 196612
  14.2 82.6 %copy-start.37 = (f32[256,64]{1,0:T(8,128)}, f32[256,64]{1,0:T(8,128)S(1)}, u32[]{:S(2)}) copy-start(f32[256,64]{1,0:T(8,128)S(1)} %get-tuple-element.128) | copy-start | bytes 196612
  109.6 498.5 %reduce-scatter.2.cloned.1.call-start = ((), (), s32[]{:S(2)}) async-start(), calls=%async_computation.7 | async-start | bytes 31457280 | tf_op jit(solution)/shard_map/reduce_scatter | solution.py:162
  129.9 39.1 %copy-start.49 = (f32[2048]{0:T(1024)S(1)}, f32[2048]{0:T(1024)}, u32[]{:S(2)}) copy-start(f32[2048]{0:T(1024)} %param.18) | copy-start | bytes 24580
  169.3 456.0 %copy-start.12 = (bf16[256,2048]{1,0:T(8,128)(2,1)}, bf16[256,2048]{1,0:T(8,128)(2,1)S(1)}, u32[]{:S(2)}) copy-start(bf16[256,2048]{1,0:T(8,128)(2,1)S(1)} %multiply_convert_fusion) | copy-start | bytes 3145732
  616.2 47.4 %all-to-all-start.1 = ((bf16[32,2,12,2048]{3,1,2,0:T(2,128)(2,1)}), bf16[32,2,12,2048]{3,1,2,0:T(2,128)(2,1)}, u32[]{:S(2)}, u32[]{:S(2)}) async-start(bf16[32,2,12,2048]{3,1,2,0:T(2,128)(2,1)} %copy.245), calls=%async_computation.2 | async-start | bytes 6291456 | tf_op jit(solution)/shard_map/all_to_all | solution.py:165
  625.3 59.4 %copy-start.60 = (pred[2048]{0:T(1024)(128)(4,1)}, pred[2048]{0:T(1024)(128)(4,1)S(1)}, u32[]{:S(2)}) copy-start(pred[2048]{0:T(1024)(128)(4,1)S(1)} %compare_and_fusion) | copy-start | bytes 6148
  625.7 43.4 %copy-start.54 = (f32[256]{0:T(256)}, f32[256]{0:T(256)S(1)}, u32[]{:S(2)}) copy-start(f32[256]{0:T(256)S(1)} %get-tuple-element.133) | copy-start | bytes 3076
  625.8 43.3 %copy-start.68 = (f32[256]{0:T(256)}, f32[256]{0:T(256)S(1)}, u32[]{:S(2)}) copy-start(f32[256]{0:T(256)S(1)} %fusion.84) | copy-start | bytes 3076
  925.1 368.5 %all-to-all-start.3 = ((f32[32,2,48,2048]{3,2,1,0:T(8,128)}), f32[32,2,48,2048]{3,2,1,0:T(8,128)}, u32[]{:S(2)}, u32[]{:S(2)}) async-start(f32[32,2,48,2048]{3,2,1,0:T(8,128)} %copy.250), calls=%async_computation.4 | async-start | bytes 50331648 | tf_op jit(solution)/shard_map/all_to_all | solution.py:200
  930.6 489.6 %all-reduce.13.cloned.1.call-start = ((), (), s32[]{:S(2)}) async-start(), calls=%async_computation.8 | async-start | bytes 2097152 | tf_op jit(solution)/shard_map/psum | solution.py:207
  932.2 395.4 %copy-start.44 = (bf16[256,64]{0,1:T(8,128)(2,1)}, bf16[256,64]{0,1:T(8,128)(2,1)S(1)}, u32[]{:S(2)}) copy-start(bf16[256,64]{0,1:T(8,128)(2,1)S(1)} %multiply_convert_fusion.4) | copy-start | bytes 98308
  1327.6 205.3 %all-reduce.17.cloned.1.call-start = ((), (), s32[]{:S(2)}) async-start(), calls=%async_computation.10 | async-start | bytes 4194304 | tf_op jit(solution)/shard_map/psum | solution.py:206
  1328.7 91.6 %copy-start.2 = (f32[256,2048]{1,0:T(8,128)S(1)}, f32[256,2048]{1,0:T(8,128)}, u32[]{:S(2)}) copy-start(f32[256,2048]{1,0:T(8,128)} %copy-done.1) | copy-start | bytes 6291460
  1328.7 91.6 %copy-start.45 = (bf16[256,64]{0,1:T(8,128)(2,1)S(1)}, bf16[256,64]{0,1:T(8,128)(2,1)}, u32[]{:S(2)}) copy-start(bf16[256,64]{0,1:T(8,128)(2,1)} %copy-done.44) | copy-start | bytes 98308
  1328.7 91.6 %copy-start.50 = (f32[2048]{0:T(1024)S(1)}, f32[2048]{0:T(1024)}, u32[]{:S(2)}) copy-start(f32[2048]{0:T(1024)} %param.18) | copy-start | bytes 24580
  1328.7 91.6 %copy-start.71 = (f32[256]{0:T(256)S(1)}, f32[256]{0:T(256)}, u32[]{:S(2)}) copy-start(f32[256]{0:T(256)} %copy-done.70) | copy-start | bytes 3076
  1339.4 83.0 %copy-start.16 = (bf16[256,2048]{1,0:T(8,128)(2,1)S(1)}, bf16[256,2048]{1,0:T(8,128)(2,1)}, u32[]{:S(2)}) copy-start(bf16[256,2048]{1,0:T(8,128)(2,1)} %param.23) | copy-start | bytes 3145732
  1459.3 209.4 %all-reduce.15.cloned.1.call-start = ((), (), s32[]{:S(2)}) async-start(), calls=%async_computation.9 | async-start | bytes 17301504
  (57 other events, 352.9 us)
Sparse Core Ops, SparseCore 0:
  10.9 55.4 all-gather.1
  109.7 56.0 all-reduce.10
  395.8 212.1 reduce-scatter.1
  1327.7 92.4 all-reduce.12
  1459.4 57.9 all-reduce.16
  1520.9 122.1 all-reduce.14
where the time goes:
time: 1690 us; the launch traced here: 1680 us
  waiting for transfers between devices  779 us (46%)
  blocking collectives  450 us (27%)
  local copies, waits for them, and re-layouts  170 us (10%)
  matrix products  141 us (8%)
  other arithmetic  110 us (7%)
    all_to_all x1, waiting for transfers between devices, body(): lax.all_to_all(d_rows, ('dp', 'expert'), split_axis=0, concat_axis=0, til...  361 us
    reduce_scatter x1, waiting for transfers between devices, body(): lax.psum_scatter(expert_part, 'mp', scatter_dimension=2, tiled=True)  212 us
    all_to_all x1, blocking collectives, body(): lax.all_to_all(send, ('dp', 'expert'), split_axis=0, concat_axis=0, tiled...  148 us
    all_to_all x1, blocking collectives, body(): lax.all_to_all(grad_send, ('dp', 'expert'), split_axis=0, concat_axis=0,...  146 us
    psum x1, blocking collectives, body(): lax.psum(grad_attn.astype(jnp.bfloat16), ('dp', 'expert'))  127 us
    psum x1, waiting for transfers between devices, body(): lax.psum(dm_part.astype(jnp.bfloat16), 'mp').astype(jnp.float32)  80.9 us
    all_gather x1, waiting for transfers between devices, body(): gathered = lax.all_gather(blocks, ('dp', 'expert'), axis=1, tiled=True)  52.1 us
    all_to_all x1, waiting for transfers between devices, body(): lax.all_to_all(expert_quarter, ('dp', 'expert'), split_axis=0, concat_axi...  37.2 us
  transfers between devices with their start and end apart: 8, of which 6 were waited for; matrix products, arithmetic and copies ran while one was open for 7% of the time, Pallas kernels for 0%

commit v1 on v0

v1 whole, which is shorter than its diff:
```python
import functools

import jax
import jax.numpy as jnp
from jax import lax
from jax.experimental import pallas as pl
from jax.experimental.pallas import tpu as pltpu
from jax.sharding import PartitionSpec as P

HEADS = 16
HEAD = 128
TOK = 256
SEQS = 4
EXPERTS = 64
CAP = 48
VMEM_LIMIT = 60 * 1024 * 1024


EPSILON = 1e-05


def dot(a, b, dims):
    return lax.dot_general(a, b, (dims, ((), ())), preferred_element_type=jnp.float32)


NN = ((1,), (0,))
NT = ((1,), (1,))
TN = ((0,), (0,))


RING = 4
X, Z, Y = 0, 1, 2


def place():
    x, e, y = (lax.axis_index(name) for name in ("dp", "expert", "mp"))
    return (x, e // 2, y), e % 2


def device_at(axis, at, core):
    return {X: {"dp": at}, Z: {"expert": at * 2 + core}, Y: {"mp": at}}[axis]


class Links:
    def __init__(self, axes, send_sems, recv_sems, pair=False, extra=()):
        self.at, self.core = place()
        self.send_sems, self.recv_sems, self.used, self.open = send_sems, recv_sems, 0, {}
        self.ended = set()
        barrier = pltpu.get_barrier_semaphore()
        peers = [self.peer(axis, step) for axis in axes for step in (1, -1)]
        peers += [self.peer(axis, step) for axis, step in extra]
        if pair:
            peers.append(self.pair())
        for peer in peers:
            pl.semaphore_signal(
                barrier, inc=1, device_id=peer, device_id_type=pl.DeviceIdType.MESH
            )
        pl.semaphore_wait(barrier, len(peers))

    def rel(self, axis, step):
        return lax.rem(self.at[axis] + (step + RING), RING)

    def peer(self, axis, step):
        return device_at(axis, self.rel(axis, step), self.core)

    def pair(self):
        return {"expert": self.at[Z] * 2 + (1 - self.core)}

    def copy(self, k, src, dst, peer):
        return pltpu.make_async_remote_copy(
            src_ref=src,
            dst_ref=dst,
            send_sem=self.send_sems.at[k],
            recv_sem=self.recv_sems.at[k],
            device_id=peer,
            device_id_type=pl.DeviceIdType.MESH,
        )

    def reserve(self):
        k = self.used
        assert k < self.send_sems.shape[0]
        self.used += 1
        return k

    def send(self, src, dst, peer, k=None):
        k = self.reserve() if k is None else k
        dst = dst() if callable(dst) else dst
        self.copy(k, src() if callable(src) else src, dst, peer).start()
        self.open[k] = src
        return k

    def sent(self, k, src):
        src = src() if callable(src) else src
        self.copy(k, src, src, self.pair()).wait_send()
        self.ended.add(k)

    def arrive(self, k, dst):
        self.copy(k, dst, dst, self.pair()).wait_recv()

    def close(self):
        for k, src in self.open.items():
            if k not in self.ended:
                self.sent(k, src)


def run_all(steps):
    steps = list(steps)
    while steps:
        steps = [s for s in steps if next(s, "end") != "end"]


def gather_part(links, view, shard, order, forward=None, late=False):
    mine = [links.at[axis] for axis in order]
    n = len(order)
    arrived = [{} for _ in order]
    held = []

    def region(i, c, step, half=None):
        places = {}
        for j, axis in enumerate(order):
            if j == i:
                places[axis] = links.rel(axis, step)
            elif j > i:
                places[axis] = mine[j]
            elif j == i - 1 and c is not None:
                places[axis] = links.rel(axis, c)
        return view(places, half)

    def own(i, c):
        if late and i == n - 1 and c not in held:
            held.append(c)
            return
        src = shard if i == 0 or (i == 1 and c == 0) else region(i, c, 0)
        for step in (1, -1):
            k = links.send(src, region(i, c, 0), links.peer(order[i], step))
            arrived[i][c, -step] = k

    def onward(i, c, step):
        links.arrive(arrived[i][c, step], region(i, c, step))
        half = 0 if step == -1 else 1
        part = region(i, c, step, half)
        arrived[i][c, 2, half] = links.send(part, part, links.peer(order[i], -step))

    def opposite(i, c):
        for half in (0, 1):
            links.arrive(arrived[i][c, 2, half], region(i, c, 2, half))

    for i in range(n):
        chunks = [None] if i == 0 else [0, -1, 1, 2]
        if late and i == n - 1:
            for c in chunks:
                own(i, c)
            yield
        if i == 0:
            own(0, None)
            if forward:
                forward(shard, region(0, None, 0))
            if n > 1:
                own(1, 0)
            yield
        for step in (-1, 1):
            for c in chunks:
                onward(i, c, step)
            if i + 1 < n:
                own(i + 1, step)
            if forward:
                forward(region(i, None, step), region(i, None, step))
            yield
        for c in chunks:
            opposite(i, c)
        if i + 1 < n:
            own(i + 1, 2)
        if i + 2 < n:
            own(i + 2, 0)
        if forward:
            forward(region(i, None, 2), region(i, None, 2))
        yield


def cut_as(*tiles):
    return [(sum(tiles[:i]) * 128, size * 128) for i, size in enumerate(tiles)]


def add_into(dst, *others):
    def one(d, *refs):
        total = d[...].astype(jnp.float32)
        for ref in refs:
            total = total + ref[...].astype(jnp.float32)
        d[...] = total.astype(d.dtype)

    if len(dst.shape) == 2:
        one(dst, *others)
    else:

        @pl.loop(0, dst.shape[0])
        def _(i):
            one(dst.at[i], *(ref.at[i] for ref in others))


def halves(ref, half):
    rows = ref.shape[-2]
    cut = pl.ds(half * (rows // 2), rows // 2)
    return ref.at[cut] if len(ref.shape) == 2 else ref.at[:, cut]


def reduce_axis(links, axis, opp, right, left, own, passing, landing, ready=None):
    to_right, to_left = links.peer(axis, 1), links.peer(axis, -1)
    k_a = links.send(halves(opp, 0), passing.at[0], to_right)
    k_b = links.send(halves(opp, 1), passing.at[1], to_left)
    k_c = links.send(halves(right[0], 1), halves(landing.at[0], 1), to_right)
    k_d = links.send(halves(left[0], 0), halves(landing.at[1], 0), to_left)
    yield
    if ready is not None:
        ready()
    links.arrive(k_a, passing.at[0])
    add_into(passing.at[0], right[1])
    k_e = links.send(passing.at[0], halves(landing.at[0], 0), to_right)
    links.arrive(k_b, passing.at[1])
    add_into(passing.at[1], left[1])
    k_f = links.send(passing.at[1], halves(landing.at[1], 1), to_left)
    yield
    links.arrive(k_c, halves(landing.at[0], 1))
    links.arrive(k_d, halves(landing.at[1], 0))
    links.arrive(k_e, halves(landing.at[0], 0))
    links.arrive(k_f, halves(landing.at[1], 1))
    add_into(own, landing.at[0], landing.at[1])


def reduce_small(links, axis, acc, own, passing, landing):
    right, left = acc(1), acc(-1)
    yield from reduce_axis(
        links,
        axis,
        acc(2),
        (right, halves(right, 0)),
        (left, halves(left, 1)),
        own,
        passing,
        landing,
    )


def rope_rows(position, freqs):
    angles = position.astype(jnp.float32) * freqs
    lane = lax.broadcasted_iota(jnp.int32, angles.shape, 1)
    sine = jnp.sin(angles)
    return jnp.cos(angles), jnp.where(lane < HEAD // 2, -sine, sine)


def swap(values):
    return pltpu.roll(values, HEAD // 2, 1)


def packed_layout(lengths):
    down = lax.broadcasted_iota(jnp.int32, (TOK, 1), 0)
    across = lax.broadcasted_iota(jnp.int32, (1, TOK), 1)
    seg_down = jnp.zeros((TOK, 1), jnp.int32)
    seg_across = jnp.zeros((1, TOK), jnp.int32)
    start = jnp.zeros((TOK, 1), jnp.int32)
    end = 0
    for k in range(SEQS - 1):
        length = lengths[0, k]
        end = end + length
        past = down >= end
        seg_down = seg_down + jnp.where(past, 1, 0)
        seg_across = seg_across + jnp.where(across >= end, 1, 0)
        start = start + jnp.where(past, length, 0)
    allowed = (seg_down == seg_across) & (across <= down)
    return down - start, allowed


def lanes_of(columns, rows):
    lane = lax.broadcasted_iota(jnp.int32, (rows, 128), 1)
    out = jnp.zeros((rows, 128), jnp.float32)
    for k, column in enumerate(columns):
        out = jnp.where(lane == k, column, out)
    return out


def start_sums(links, columns, sums, landing):
    sums[...] = lanes_of(columns, TOK).T[: sums.shape[0]]
    return [links.send(sums, landing.at[k], links.peer(Y, k + 1)) for k in range(3)]


def end_sums(links, sent, sums, landing):
    total = sums[...]
    for k in range(3):
        links.arrive(sent[k], landing.at[k])
        total = total + landing[k]
    fill = jnp.zeros((128 - total.shape[0], TOK), jnp.float32)
    return jnp.concatenate([total, fill], axis=0).T


def front_kernel(
    cuts,
    cot_cuts,
    lengths,
    blocks,
    tokens,
    attn_norm,
    q_gain,
    k_gain,
    ffn_norm,
    router,
    ids,
    freqs,
    cot,
    all_weights,
    rows_out,
    cot_out,
    normed,
    heads,
    raw,
    stats,
    lse,
    mixed,
    resid,
    probs_out,
    weights,
    sums,
    sums_in,
    parts,
    passing,
    landing,
    shard,
    send_sems,
    recv_sems,
    local_sems,
):
    f32, bf16 = jnp.float32, jnp.bfloat16
    links = Links((X, Z, Y), send_sems, recv_sems, pair=True, extra=[(Y, 2)])
    x, z, y = links.at
    core = links.core
    own_block = pltpu.make_async_copy(blocks, weights.at[x, z, core], local_sems.at[0])
    own_block.start()
    half_cols = blocks.shape[1] // 2
    given = []

    def view(cols, places, half):
        index = tuple(places.get(axis, slice(None)) for axis in (X, Z))
        n = blocks.shape[0] // 2
        cut = slice(None) if half is None else pl.ds(half * n, n)
        return weights.at[index + (core, cut, cols)]

    def forward(src, dst):
        given.append((links.send(src, dst, links.pair()), dst))

    gathers = [
        gather_part(
            links,
            functools.partial(view, pl.ds(part * half_cols, half_cols)),
            blocks.at[:, pl.ds(part * half_cols, half_cols)],
            order,
            forward,
        )
        for part, order in enumerate(((X, Z), (Z, X)))
    ]
    for gather in gathers:
        next(gather)

    quarter = TOK // RING

    def rows_view(out, cols, places, half):
        index = tuple(places.get(axis, slice(None)) for axis in (X, Z, Y))
        n = quarter // 2
        cut = slice(None) if half is None else pl.ds(half * n, n)
        return out.at[index + (cut, cols)]

    def row_gathers(out, source, cuts, late):
        return [
            gather_part(
                links,
                functools.partial(rows_view, out, pl.ds(start, size)),
                source.at[:, pl.ds(start, size)],
                order,
                late=order[2] in late,
            )
            for (start, size), order in zip(cuts, ((X, Z, Y), (Z, Y, X), (Y, X, Z)))
        ]

    cot_mine = cot.at[pl.ds(pl.multiple_of(y * quarter, quarter), quarter)]
    cot_here = pltpu.make_async_copy(cot_mine, cot_out.at[x, z, y], local_sems.at[2])
    cot_here.start()
    cot_gathers = row_gathers(cot_out, cot_mine, cot_cuts, (X, Z, Y))
    for gather in cot_gathers:
        next(gather)
    hidden = tokens[...].astype(f32)
    attn_inv = lax.rsqrt(jnp.mean(hidden * hidden, axis=-1, keepdims=True) + EPSILON)
    normed[...] = (hidden * attn_inv * attn_norm[...]).astype(bf16)
    position, allowed = packed_layout(lengths)
    cosine, sine = rope_rows(position, freqs[...])
    cot_here.wait()
    for _ in range(6):
        for gather in gathers + cot_gathers:
            next(gather, None)
    run_all(gathers)
    for k, dst in given:
        links.arrive(k, dst)
    own_block.wait()
    for gather in cot_gathers[1:]:
        next(gather)
    save = pltpu.make_async_copy(weights, all_weights, local_sems.at[0])
    save.start()

    cols = q_gain.shape[1]
    width = tokens.shape[1]

    def project(j):
        w = weights[:, :, :, :, j * cols : (j + 1) * cols].reshape(width, cols)
        return dot(normed[...], w, NN)

    squares = []
    for j in range(2):
        value = project(j)
        raw[:, j * cols : (j + 1) * cols] = value
        squares.append(jnp.sum(value * value, axis=-1, keepdims=True))
    sent = start_sums(links, squares, sums, sums_in)
    heads[:, 2 * cols :] = project(2).astype(bf16)
    total = end_sums(links, sent, sums, sums_in)
    inverse = lax.rsqrt(total / (HEADS * HEAD) + EPSILON)
    stats[...] = inverse
    top_sums = []
    for h in range(cols // HEAD):
        own = slice(h * HEAD, (h + 1) * HEAD)
        rotated = []
        for j, gain in enumerate((q_gain, k_gain)):
            part = raw[:, j * cols + h * HEAD : j * cols + (h + 1) * HEAD]
            part = part * inverse[:, j : j + 1] * gain[:, own]
            part = (part * cosine + swap(part) * sine).astype(bf16)
            heads[:, j * cols + h * HEAD : j * cols + (h + 1) * HEAD] = part
            rotated.append(part)
        scores = dot(rotated[0], rotated[1], NT) * HEAD ** (-0.5)
        scores = jnp.where(allowed, scores, -1e30)
        top = jnp.max(scores, axis=-1, keepdims=True)
        log_total = top + jnp.log(jnp.sum(jnp.exp(scores - top), axis=-1, keepdims=True))
        top_sums.append(log_total)
        probs = jnp.exp(scores - log_total).astype(bf16)
        value = heads[:, 2 * cols + h * HEAD : 2 * cols + (h + 1) * HEAD]
        mixed[:, own] = dot(probs, value, NN).astype(bf16)
    lse[...] = lanes_of(top_sums, TOK)

    out_w = weights[:, :, :, :, 3 * cols :].reshape(width, cols)
    def quarter_rows(step):
        return pl.ds(pl.multiple_of(links.rel(Y, step) * quarter, quarter), quarter)

    for k, step in enumerate((2, 1, -1)):
        parts[k] = dot(mixed[quarter_rows(step), :], out_w, NT).astype(bf16)
    by_step = {2: parts.at[0], 1: parts.at[1], -1: parts.at[2]}
    summing = reduce_small(links, Y, by_step.get, resid, passing, landing)
    next(summing)
    rows = quarter_rows(0)
    resid[...] = tokens[rows, :].astype(f32) + dot(mixed[rows, :], out_w, NT)
    run_all([summing])
    total = resid[...]
    ffn_inv = lax.rsqrt(jnp.mean(total * total, axis=-1, keepdims=True) + EPSILON)
    moe_in = (total * ffn_inv * ffn_norm[...]).astype(bf16)
    logits = dot(moe_in, router[...], NN)
    logits = logits - jnp.max(logits, axis=-1, keepdims=True)
    chances = jnp.exp(logits)
    chances = chances / jnp.sum(chances, axis=-1, keepdims=True)
    mine = ids[rows, :]
    expert = lax.broadcasted_iota(jnp.int32, chances.shape, 1)
    picks = jnp.zeros(chances.shape, f32)
    for k in range(ids.shape[1]):
        picks = picks + jnp.where(mine[:, k : k + 1] == expert, 1.0, 0.0)
    both = jnp.concatenate([chances, picks], axis=1)
    probs_out[...] = both
    shard[:, :width] = moe_in
    shard[:, width:] = both.astype(bf16)
    here = pltpu.make_async_copy(shard, rows_out.at[x, z, y], local_sems.at[1])
    here.start()

    gathers = row_gathers(rows_out, shard, cuts, ())
    last_y, others = cot_gathers[0], cot_gathers[1:]

    def step(parts, count=1):
        for _ in range(count):
            for part in parts:
                next(part, None)

    step(gathers)
    here.wait()
    step(others, 2)
    step([last_y])
    step(gathers, 6)
    step(others)
    step([last_y], 2)
    step(gathers, 2)
    run_all([last_y] + others + gathers)
    save.wait()
    links.close()


def front(
    lengths, blocks, tokens, attn_norm, q_gain, k_gain, ffn_norm, router, ids, cot, collective_id
):
    bf16, f32 = jnp.bfloat16, jnp.float32
    block_rows, wide = blocks.shape
    rows, width = tokens.shape
    cols = q_gain.shape[1]
    quarter = rows // RING
    ext = width + 128
    half = HEAD // 2
    freqs = 10000.0 ** (-jnp.arange(half, dtype=f32) / half)
    freqs = jnp.concatenate([freqs, freqs])[None, :]
    in_vmem = pl.BlockSpec(memory_space=pltpu.VMEM)
    in_hbm = pl.BlockSpec(memory_space=pltpu.HBM)
    shape = jax.ShapeDtypeStruct
    return pl.pallas_call(
        functools.partial(front_kernel, cut_as(4, 6, 7), cut_as(4, 6, 6)),
        in_specs=[pl.BlockSpec(memory_space=pltpu.SMEM), in_hbm] + [in_vmem] * 8 + [in_hbm],
        out_specs=[in_hbm, in_hbm, in_hbm] + [in_vmem] * 8,
        out_shape=[
            shape((RING, RING, 2, block_rows, wide), bf16),
            shape((RING, RING, RING, quarter, ext), bf16),
            shape((RING, RING, RING, quarter, width), bf16),
            shape((rows, width), bf16),
            shape((rows, 3 * cols), bf16),
            shape((rows, 2 * cols), f32),
            shape((rows, 128), f32),
            shape((rows, 128), f32),
            shape((rows, cols), bf16),
            shape((quarter, width), f32),
            shape((quarter, 128), f32),
        ],
        scratch_shapes=[
            pltpu.VMEM((RING, RING, 2, block_rows, wide), bf16),
            pltpu.VMEM((8, rows), f32),
            pltpu.VMEM((3, 8, rows), f32),
            pltpu.VMEM((3, quarter, width), bf16),
            pltpu.VMEM((2, quarter // 2, width), bf16),
            pltpu.VMEM((2, quarter, width), bf16),
            pltpu.VMEM((quarter, ext), bf16),
            pltpu.SemaphoreType.DMA((282,)),
            pltpu.SemaphoreType.DMA((282,)),
            pltpu.SemaphoreType.DMA((3,)),
        ],
        compiler_params=pltpu.CompilerParams(
            collective_id=collective_id, has_side_effects=True, vmem_limit_bytes=VMEM_LIMIT
        ),
        cost_estimate=pl.CostEstimate(flops=0, bytes_accessed=0, transcendentals=0),
        name="front",
    )(lengths, blocks, tokens, attn_norm, q_gain, k_gain, ffn_norm, router, ids, freqs, cot)


ORDER = (2, 1, -1, 0)


def far_first(i):
    return 2 - i + 3 * (i * (i - 1) // 2)


PLAN = {
    (1, 0): (
        (0, 0, 0, 0, 0),
        (0, 1, 0, 0, 0),
        (0, 0, 1, 0, 0),
        (0, 1, 0, 1, 0),
    ),
    (2, 0): (
        (0, 2, 0, 0, 0),
        (0, 0, 2, 0, 0),
        (0, 0, 3, 0, 0),
        (0, 1, 0, 1, 1),
        (0, 2, 0, 1, 0),
        (0, 2, 0, 1, 1),
    ),
    (2, 1): (
        (0, 1, 0, 2, 0),
        (0, 1, 0, 2, 1),
    ),
    (3, 0): (
        (0, 1, 0, 3, 0),
        (0, 1, 0, 3, 1),
        (0, 1, 1, 0, 0),
        (0, 0, 0, 1, 0),
        (0, 0, 0, 2, 0),
        (0, 2, 0, 2, 0),
        (0, 2, 0, 2, 1),
        (0, 0, 1, 1, 0),
        (0, 0, 1, 2, 0),
        (0, 1, 1, 1, 0),
    ),
    (3, 1): (
        (0, 0, 0, 3, 0),
        (0, 2, 0, 3, 0),
        (0, 2, 0, 3, 1),
        (0, 0, 1, 3, 0),
    ),
    (4, 0): (
        (0, 1, 0, 4, 0),
        (0, 2, 1, 0, 0),
        (0, 1, 1, 1, 1),
        (0, 2, 1, 1, 0),
        (0, 2, 1, 1, 1),
        (0, 0, 2, 1, 0),
        (0, 0, 3, 1, 0),
    ),
    (4, 1): (
        (0, 1, 0, 5, 0),
        (1, 1, 0, 0, 0),
        (0, 2, 0, 4, 0),
        (0, 1, 1, 2, 0),
        (0, 1, 1, 2, 1),
    ),
    (5, 0): (
        (0, 2, 0, 5, 0),
        (1, 2, 0, 0, 0),
        (0, 2, 1, 2, 0),
        (0, 2, 1, 2, 1),
        (0, 0, 2, 2, 0),
        (0, 1, 1, 3, 0),
        (0, 0, 3, 2, 0),
        (0, 1, 1, 3, 1),
        (0, 1, 2, 0, 0),
        (0, 0, 0, 1, 1),
        (0, 0, 0, 2, 1),
        (0, 0, 1, 1, 1),
        (0, 0, 1, 2, 1),
        (0, 1, 2, 1, 0),
    ),
    (5, 1): (
        (0, 0, 0, 3, 1),
        (0, 0, 1, 3, 1),
        (0, 2, 1, 3, 0),
        (0, 2, 1, 3, 1),
        (0, 0, 2, 3, 0),
        (0, 0, 3, 3, 0),
    ),
    (6, 0): (
        (0, 1, 1, 4, 0),
        (0, 2, 2, 0, 0),
        (0, 0, 2, 1, 1),
        (0, 1, 2, 1, 1),
        (0, 2, 2, 1, 0),
        (0, 2, 2, 1, 1),
        (0, 0, 3, 1, 1),
    ),
    (6, 1): (
        (0, 1, 1, 5, 0),
        (0, 2, 1, 4, 0),
        (1, 1, 0, 3, 0),
        (0, 1, 2, 2, 0),
        (0, 1, 2, 2, 1),
    ),
    (7, 0): (
        (0, 2, 1, 5, 0),
        (1, 2, 0, 3, 0),
        (0, 0, 0, 4, 0),
        (0, 0, 2, 2, 1),
        (0, 2, 2, 2, 0),
        (0, 2, 2, 2, 1),
        (0, 1, 2, 3, 0),
        (0, 1, 2, 3, 1),
        (0, 1, 3, 0, 0),
        (0, 1, 3, 1, 0),
    ),
    (7, 1): (
        (0, 0, 0, 5, 0),
        (1, 0, 0, 0, 0),
        (0, 0, 1, 4, 0),
        (0, 0, 3, 2, 1),
        (0, 0, 2, 3, 1),
        (0, 2, 2, 3, 0),
        (0, 2, 2, 3, 1),
    ),
    (8, 0): (
        (0, 0, 1, 5, 0),
        (0, 1, 2, 4, 0),
        (0, 0, 3, 3, 1),
        (0, 2, 3, 0, 0),
        (0, 1, 3, 1, 1),
        (0, 2, 3, 1, 0),
        (0, 2, 3, 1, 1),
        (0, 1, 2, 5, 0),
        (1, 1, 0, 3, 1),
        (0, 1, 3, 2, 0),
        (0, 1, 3, 2, 1),
        (0, 2, 2, 4, 0),
        (0, 1, 3, 3, 0),
        (0, 1, 3, 3, 1),
        (0, 0, 2, 4, 0),
        (0, 2, 2, 5, 0),
        (1, 2, 0, 3, 1),
        (0, 0, 2, 5, 0),
        (1, 0, 0, 3, 1),
        (3, 0, 0, 0, 0),
        (0, 0, 3, 4, 0),
        (0, 2, 3, 2, 0),
        (0, 2, 3, 2, 1),
        (3, 0, 0, 0, 0),
        (0, 0, 3, 5, 0),
        (0, 2, 3, 3, 0),
        (0, 2, 3, 3, 1),
        (1, 0, 0, 3, 0),
        (3, 0, 0, 0, 0),
        (3, 0, 0, 0, 0),
        (0, 1, 3, 4, 0),
        (3, 0, 0, 0, 0),
        (0, 1, 3, 5, 0),
        (1, 1, 0, 5, 0),
        (2, 1, 0, 0, 0),
        (3, 0, 0, 0, 0),
        (0, 2, 3, 4, 0),
        (2, 1, 0, 3, 0),
        (2, 1, 0, 3, 1),
        (0, 2, 3, 5, 0),
        (1, 0, 0, 5, 0),
        (2, 0, 0, 0, 0),
        (3, 0, 0, 0, 0),
        (2, 1, 0, 5, 0),
        (2, 0, 0, 3, 0),
        (2, 0, 0, 3, 1),
        (3, 0, 0, 0, 0),
        (1, 2, 0, 5, 0),
        (2, 2, 0, 0, 0),
        (2, 0, 0, 5, 0),
        (3, 0, 0, 0, 0),
        (2, 2, 0, 3, 0),
        (2, 2, 0, 3, 1),
        (3, 0, 0, 0, 0),
        (3, 0, 0, 0, 0),
        (2, 2, 0, 5, 0),
    ),
}


class RingSum:
    def __init__(self, links, axis, term, passed, landed, side, stage, own, final, sems, before):
        self.links, self.axis, self.term = links, axis, term
        self.passed, self.landed, self.side, self.stage = passed, landed, side, stage
        self.own, self.final, self.sems, self.before = own, final, sems, before
        self.k = {(n, d): links.reserve() for n in ("pass", "direct", "sum") for d in (0, 1)}

    def first(self):
        for d, step in enumerate((1, -1)):
            self.links.send(
                functools.partial(self.term, 2, d),
                functools.partial(self.passed, d),
                self.links.peer(self.axis, step),
                self.k["pass", d],
            )

    def direct(self, d):
        step = (1, -1)[d]
        self.links.send(
            functools.partial(self.term, step, 1 - d),
            lambda: halves(self.landed(d), 1 - d),
            self.links.peer(self.axis, step),
            self.k["direct", d],
        )

    def side_load(self, d):
        return pltpu.make_async_copy(
            self.term((1, -1)[d], d), self.side.at[d], self.sems.at[d]
        )

    def stage_load(self, d):
        return pltpu.make_async_copy(self.passed(d), self.stage.at[d], self.sems.at[2 + d])

    def prepare(self, d):
        self.side_load(d).start()
        if self.before is not None:
            self.links.sent(self.before.k["sum", d], self.stage.at[d])
        self.links.arrive(self.k["pass", d], self.passed(d))
        self.stage_load(d).start()

    def onward(self, d):
        self.side_load(d).wait()
        self.stage_load(d).wait()
        add_into(self.stage.at[d], self.side.at[d])
        self.links.send(
            lambda: self.stage.at[d],
            lambda: halves(self.landed(d), d),
            self.links.peer(self.axis, (1, -1)[d]),
            self.k["sum", d],
        )

    def own_load(self):
        return pltpu.make_async_copy(self.term(0, None), self.own, self.sems.at[4])

    def final_load(self, d):
        return pltpu.make_async_copy(self.landed(d), self.final.at[d], self.sems.at[5 + d])

    def collect(self):
        self.own_load().start()
        for d in (0, 1):
            self.links.arrive(self.k["direct", d], halves(self.landed(d), 1 - d))
            self.links.arrive(self.k["sum", d], halves(self.landed(d), d))
            self.final_load(d).start()

    def finish(self):
        self.own_load().wait()
        for d in (0, 1):
            self.final_load(d).wait()
        add_into(self.own, self.final.at[0], self.final.at[1])


class NearSum:
    def __init__(self, links, axis, acc, passing, landing):
        self.links, self.axis, self.acc = links, axis, acc
        self.passing, self.landing = passing, landing
        self.k = {(n, d): links.reserve() for n in ("pass", "direct", "sum") for d in (0, 1)}

    def first(self):
        for d, step in enumerate((1, -1)):
            self.links.send(
                lambda d=d: halves(self.acc(2), d),
                lambda d=d: self.passing.at[d],
                self.links.peer(self.axis, step),
                self.k["pass", d],
            )

    def onward(self, d):
        step = (1, -1)[d]
        peer = self.links.peer(self.axis, step)
        self.links.send(
            lambda: halves(self.acc(step), 1 - d),
            lambda: halves(self.landing.at[d], 1 - d),
            peer,
            self.k["direct", d],
        )
        self.links.arrive(self.k["pass", d], self.passing.at[d])
        add_into(self.passing.at[d], halves(self.acc(step), d))
        self.links.send(
            lambda: self.passing.at[d],
            lambda: halves(self.landing.at[d], d),
            peer,
            self.k["sum", d],
        )

    def finish(self):
        for d in (0, 1):
            self.links.arrive(self.k["direct", d], halves(self.landing.at[d], 1 - d))
            self.links.arrive(self.k["sum", d], halves(self.landing.at[d], d))
        add_into(self.acc(0), self.landing.at[0], self.landing.at[1])


def experts_kernel(
    cuts,
    x_all,
    dy_all,
    w_own,
    w_pair,
    resid,
    chances,
    router,
    ffn_norm,
    cot,
    d_resid,
    out_mine,
    d_resid_mine,
    small_rows,
    grad_experts,
    grad_down,
    xs,
    ds,
    act,
    ret,
    pair_in,
    *refs,
):
    f32, bf16 = jnp.float32, jnp.bfloat16
    hbm, refs = refs[:6], refs[6:]
    bufs, refs = refs[:27], refs[27:]
    (
        home,
        stage,
        cot_now,
        send_sems,
        recv_sems,
        ring_sems,
        load_sems,
        store_sems,
        weight_sems,
        cot_sem,
        grad_load_sems,
        grad_pair_sems,
        grad_store_sems,
    ) = refs
    links = Links((X, Z, Y), send_sems, recv_sems, pair=True)
    here_x, here_z, here_y = links.at
    rows = ret.shape[3]
    width = resid.shape[1]
    ff = act.shape[2] // 3
    cap = CAP
    locals_ = xs.shape[0]
    half_experts = locals_ // 2
    group = (here_x * RING + here_z) * 2
    ids = [(group + links.core) * half_experts + j for j in range(half_experts)]
    ids += [(group + 1 - links.core) * half_experts + j for j in range(half_experts)]

    cot_rows = cot.at[pl.ds(pl.multiple_of(here_y * rows, rows), rows)]
    cot_load = pltpu.make_async_copy(cot_rows, cot_now, cot_sem)
    cot_load.start()

    def group_at(s, g):
        gx = lax.rem(here_x + far_first(s // 2) + RING, RING)
        gz = lax.rem(here_z + far_first(2 * (s % 2) + g) + RING, RING)
        return gx, gz

    orders = ((X, Z, Y), (Z, X, Y), (Y, X, Z))
    far, near, last = [], [], []
    for p, ((start, size), (a1, a2, a3)) in enumerate(zip(cuts, orders)):
        side, stg, acc, final, pass_b, land_b, pass_c, land_c, _ = bufs[9 * p : 9 * p + 9]
        passed, landed = hbm[2 * p : 2 * p + 2]

        def term(a1, a2, c, start, size, step, half):
            places = {a1: links.rel(a1, step), a2: links.rel(a2, ORDER[c])}
            index = tuple(places.get(axis, slice(None)) for axis in (X, Z, Y))
            cut = slice(None) if half is None else pl.ds(half * (rows // 2), rows // 2)
            return ret.at[index + (cut, pl.ds(start, size))]

        slots = side.shape[0]
        chunks = []
        for c in range(4):
            chunks.append(
                RingSum(
                    links,
                    a1,
                    functools.partial(term, a1, a2, c, start, size),
                    lambda d, passed=passed, c=c: passed.at[d, c],
                    lambda d, landed=landed, c=c: landed.at[d, c],
                    side.at[c % slots],
                    stg.at[c % slots],
                    acc.at[c],
                    final,
                    ring_sems.at[p, c],
                    chunks[c - slots] if c >= slots else None,
                )
            )
        far.append(chunks)
        near.append(
            NearSum(links, a2, lambda step, acc=acc: acc.at[ORDER.index(step)], pass_b, land_b)
        )
        last.append(
            NearSum(
                links,
                a3,
                lambda step, acc=acc, a3=a3: acc.at[3, links.rel(a3, step)],
                pass_c,
                land_c,
            )
        )

    rings = (far, near, last)

    def act_at(key, work=None):
        for kind, p, c, method, d in PLAN.get(key, ()):
            if kind == 3:
                next(work, None)
                continue
            ring = far[p][c] if kind == 0 else rings[kind][p]
            name = ("first", "direct", "prepare", "onward", "collect", "finish")[method]
            call = getattr(ring, name)
            call(d) if method in (1, 2, 3) else call()

    lane = lax.broadcasted_iota(jnp.int32, (2 * locals_, 128), 1)
    row = lax.broadcasted_iota(jnp.int32, (2 * locals_, 128), 0)
    select = jnp.zeros((2 * locals_, 128), f32)
    for j in range(locals_):
        select = jnp.where((row == j) & (lane == ids[j] + EXPERTS), 1.0, select)
        select = jnp.where((row == locals_ + j) & (lane == ids[j]), 1.0, select)
    select = select.astype(bf16)
    before = jnp.where(
        lax.broadcasted_iota(jnp.int32, (TOK, TOK), 0)
        < lax.broadcasted_iota(jnp.int32, (TOK, TOK), 1),
        1.0,
        0.0,
    ).astype(bf16)
    slots = lax.broadcasted_iota(jnp.int32, (cap, TOK), 0).astype(f32)
    out_lane = lax.broadcasted_iota(jnp.int32, (2 * cap, 128), 1)
    def groups(weights, x, dy, xs_now, ds_now, act_now, terms, ret_now):
        def weight_loads():
            return [
                pltpu.make_async_copy(w_own, weights.at[0], weight_sems.at[0]),
                pltpu.make_async_copy(w_pair, weights.at[1], weight_sems.at[1]),
            ]

        for copy in weight_loads():
            copy.start()

        def loads(s):
            copies = []
            for g in range(2):
                gx, gz = group_at(s, g)
                copies.append(pltpu.make_async_copy(x_all.at[gx, gz], x.at[g], load_sems.at[g, 0]))
                copies.append(pltpu.make_async_copy(dy_all.at[gx, gz], dy.at[g], load_sems.at[g, 1]))
            return copies

        def rows_of(s):
            start = s * 2 * cap
            return pl.ds(start if isinstance(s, int) else pl.multiple_of(start, 2 * cap), 2 * cap)

        def row_stores(s):
            at = rows_of(s)
            return [
                pltpu.make_async_copy(xs_now, xs.at[:, at], store_sems.at[0]),
                pltpu.make_async_copy(ds_now, ds.at[:, at], store_sems.at[1]),
            ]

        def act_store(s):
            at = rows_of(s)
            return pltpu.make_async_copy(act_now, act.at[:, at], store_sems.at[2])

        def ret_store(s, g):
            gx, gz = group_at(s, g)
            return pltpu.make_async_copy(ret_now.at[g], ret.at[gx, gz], store_sems.at[3 + g])

        for copy in loads(0):
            copy.start()

        @pl.loop(0, 8)
        def _(s):
            places, gates = [], []
            for copy in loads(s):
                copy.wait()

            @pl.when(s > 0)
            def _():
                for copy in row_stores(s):
                    copy.wait()

            for g in range(2):
                marks = x[g, :, :, width:].reshape(TOK, 128)
                flags = dot(select, marks, NT)
                slot = dot(flags.astype(bf16), before, NN)
                place, gate = [], []
                for j in range(locals_):
                    hit = (slots == slot[j : j + 1]) & (flags[j : j + 1] > 0.5)
                    place.append(jnp.where(hit, 1.0, 0.0))
                    gate.append(
                        jnp.sum(place[-1] * flags[locals_ + j : locals_ + j + 1], axis=1, keepdims=True)
                    )
                place = jnp.concatenate(place, axis=0).astype(bf16)
                places.append(place)
                gates.append(gate)
                picked = dot(place, x[g, :, :, :width].reshape(TOK, width), NN).astype(bf16)
                picked_dy = dot(place, dy[g].reshape(TOK, width), NN).astype(bf16)
                for j in range(locals_):
                    xs_now[j, g * cap : (g + 1) * cap, :] = picked[j * cap : (j + 1) * cap]
                    ds_now[j, g * cap : (g + 1) * cap, :] = picked_dy[j * cap : (j + 1) * cap]
            for copy in row_stores(s):
                copy.start()

            @pl.when(s < 7)
            def _():
                for copy in loads(s + 1):
                    copy.start()

            @pl.when(s == 0)
            def _():
                for copy in weight_loads():
                    copy.wait()

            @pl.when(s > 0)
            def _():
                act_store(s).wait()
                for g in range(2):
                    ret_store(s, g).wait()

            for k in range(1, 8):
                pl.when(s == k)(functools.partial(act_at, (k, 0)))

            for j in range(locals_):
                if j == half_experts:
                    for k in range(1, 8):
                        pl.when(s == k)(functools.partial(act_at, (k, 1)))
                w = weights.at[j // half_experts, j % half_experts]
                gate = jnp.concatenate([gates[g][j] for g in range(2)], axis=0)
                up_in = dot(xs_now[j], w[0], NN)
                up = dot(xs_now[j], w[1], NN)
                d_raw = dot(ds_now[j], w[2], NN)
                sig = 1.0 / (1.0 + jnp.exp(-up_in))
                silu = up_in * sig
                hidden = (silu * up).astype(bf16).astype(f32)
                d_gate = jnp.sum(hidden * d_raw, axis=1, keepdims=True)
                gated = (hidden * gate).astype(bf16)
                d_hidden = d_raw * gate
                d_up_in = (d_hidden * up * sig * (1.0 + up_in * (1.0 - sig))).astype(bf16)
                d_up = (d_hidden * silu).astype(bf16)
                act_now[j, :, :ff] = gated
                act_now[j, :, ff : 2 * ff] = d_up_in
                act_now[j, :, 2 * ff :] = d_up
                y = dot(gated, w[2], NT).astype(bf16)
                dx = (dot(d_up_in, w[0], NT) + dot(d_up, w[1], NT)).astype(bf16)
                dg = jnp.where(out_lane == ids[j], d_gate, 0.0).astype(bf16)
                for g in range(2):
                    part = slice(g * cap, (g + 1) * cap)
                    there = slice(j * cap, (j + 1) * cap)
                    terms[g, there, :width] = y[part]
                    terms[g, there, width : 2 * width] = dx[part]
                    terms[g, there, 2 * width :] = dg[part]
            act_store(s).start()
            for g in range(2):
                for start, size in cuts:
                    cut = slice(start, start + size)
                    ret_now[g, :, :, cut] = (
                        dot(places[g], terms[g, :, cut], TN).astype(bf16).reshape(RING, rows, size)
                    )
                ret_store(s, g).start()

        for g in range(2):
            ret_store(0, g).wait()
        for copy in row_stores(0) + [act_store(0)]:
            copy.wait()

    wide = x_all.shape[4]
    pl.run_scoped(
        groups,
        pltpu.VMEM((2,) + w_own.shape, bf16),
        pltpu.VMEM((2, RING, rows, wide), bf16),
        pltpu.VMEM((2, RING, rows, width), bf16),
        pltpu.VMEM((locals_, 2 * cap, width), bf16),
        pltpu.VMEM((locals_, 2 * cap, width), bf16),
        pltpu.VMEM((locals_, 2 * cap, 3 * ff), bf16),
        pltpu.VMEM((2, locals_ * cap, ret.shape[4]), bf16),
        pltpu.VMEM((2, RING, rows, ret.shape[4]), bf16),
    )

    def ending(xs_e, ds_e, act_e, given, taken, summed):
        def loads(j):
            e = (j + half_experts) % locals_
            return [
                pltpu.make_async_copy(src.at[e], dst.at[j % 2], grad_load_sems.at[j % 2, i])
                for i, (src, dst) in enumerate(((xs, xs_e), (ds, ds_e), (act, act_e)))
            ]

        def take(n):
            return pltpu.make_async_copy(
                pair_in.at[n // 3, n % 3], taken.at[n % 2], grad_pair_sems.at[n % 2]
            )

        def store(n):
            e, i = n // 3, n % 3
            dst = grad_down.at[e] if i == 2 else grad_experts.at[e, i]
            return pltpu.make_async_copy(summed.at[n % 2], dst, grad_store_sems.at[n % 2])

        sent = []

        def work():
            for copy in loads(0):
                copy.start()
            for j in range(locals_):
                for copy in loads(j):
                    copy.wait()
                if j + 1 < locals_:
                    for copy in loads(j + 1):
                        copy.start()
                for i in range(3):
                    rows_in = ds_e if i == 2 else xs_e
                    cols_in = (slice(ff, 2 * ff), slice(2 * ff, 3 * ff), slice(0, ff))[i]
                    n = (j % half_experts) * 3 + i
                    own = j >= half_experts
                    if own:
                        links.arrive(sent[n], pair_in.at[n // 3, n % 3])
                        take(n).start()
                        if n >= 2:
                            store(n - 2).wait()
                        take(n).wait()

                    @pl.loop(0, RING)
                    def _(q):
                        cut = pl.ds(pl.multiple_of(q * (width // RING), width // RING), width // RING)
                        part = dot(rows_in[j % 2, :, cut], act_e[j % 2, :, cols_in], TN)
                        if own:
                            summed[n % 2, cut, :] = part + taken[n % 2, cut, :].astype(f32)
                        else:
                            given[n, cut, :] = part.astype(bf16)

                    if own:
                        store(n).start()
                    else:
                        sent.append(
                            links.send(given.at[n], pair_in.at[n // 3, n % 3], links.pair())
                        )
                    yield

        piece = work()
        act_at((8, 0), piece)
        go_on()
        for _ in piece:
            pass
        for n in (3 * half_experts - 2, 3 * half_experts - 1):
            store(n).wait()
        for k in sent:
            links.sent(k, given.at[0])
        links.close()

    def go_on():
        for p, (start, size) in enumerate(cuts):
            acc = bufs[9 * p + 2]
            home[:, start : start + size] = acc[3, links.at[orders[p][2]]]
        cot_load.wait()

        values = resid[...]
        inverse = lax.rsqrt(jnp.mean(values * values, axis=-1, keepdims=True) + EPSILON)
        hat = values * inverse
        moe_in = (hat * ffn_norm[...]).astype(bf16)
        probs, picks = chances[:, :EXPERTS], chances[:, EXPERTS:]
        d_probs = home[:, 2 * width : 2 * width + EXPERTS].astype(f32) * picks
        d_logits = probs * (d_probs - jnp.sum(probs * d_probs, axis=-1, keepdims=True))
        d_logits = d_logits.astype(bf16)
        d_moe = home[:, width : 2 * width].astype(f32) + dot(d_logits, router[...], NT)
        d_hat = d_moe * ffn_norm[...]
        final = cot_now[...].astype(f32) + inverse * (
            d_hat - hat * jnp.mean(d_hat * hat, axis=-1, keepdims=True)
        )
        d_resid_mine[...] = final
        stage[...] = final.astype(bf16)
        here = pl.ds(pl.multiple_of(here_y * rows, rows), rows)
        copy = pltpu.make_async_copy(stage, d_resid.at[here], cot_sem)
        copy.start()

        def view(places, half):
            start = places[Y] * rows + (0 if half is None else half * (rows // 2))
            size = rows if half is None else rows // 2
            return d_resid.at[pl.ds(pl.multiple_of(start, size), size)]

        sharing = gather_part(links, view, stage, (Y,))
        next(sharing)
        out_mine[...] = (values + home[:, :width].astype(f32)).astype(bf16)
        small_rows[:EXPERTS, :] = dot(d_logits, moe_in, TN)
        row = lax.broadcasted_iota(jnp.int32, (8, width), 0)
        d_ffn = jnp.sum(d_moe * hat, axis=0, keepdims=True)
        small_rows[EXPERTS:, :] = jnp.where(row == 1, d_ffn, 0.0)
        run_all([sharing])
        copy.wait()

    chunk = xs.shape[1:]
    pl.run_scoped(
        ending,
        pltpu.VMEM((2,) + chunk, bf16),
        pltpu.VMEM((2,) + chunk, bf16),
        pltpu.VMEM((2,) + act.shape[1:], bf16),
        pltpu.VMEM((3 * half_experts, width, ff), bf16),
        pltpu.VMEM((2, width, ff), bf16),
        pltpu.VMEM((2, width, ff), f32),
    )


def experts(x_all, dy_all, w_own, w_pair, resid, chances, router, ffn_norm, cot, collective_id):
    rows, wide = x_all.shape[3:]
    width = dy_all.shape[4]
    ff = w_own.shape[3]
    locals_ = 2 * w_own.shape[0]
    groups = RING * RING
    bf16, f32 = jnp.bfloat16, jnp.float32
    cols = 2 * width + 128
    cuts = cut_as(9, 11, 13)
    vmem, dma = pltpu.VMEM, pltpu.SemaphoreType.DMA
    bufs, hbm_out = [], []
    shape = jax.ShapeDtypeStruct
    for p, (_, size) in enumerate(cuts):
        slots = 2 if p == 0 else 1
        hbm_out += [
            shape((2, 4, RING, rows // 2, size), bf16),
            shape((2, 4, RING, rows, size), bf16),
        ]
        bufs += [
            vmem((slots, 2, RING, rows // 2, size), bf16),
            vmem((slots, 2, RING, rows // 2, size), bf16),
            vmem((4, RING, rows, size), bf16),
            vmem((2, RING, rows, size), bf16),
            vmem((2, RING, rows // 2, size), bf16),
            vmem((2, RING, rows, size), bf16),
            vmem((2, rows // 2, size), bf16),
            vmem((2, rows, size), bf16),
            vmem((8, 128), bf16),
        ]
    in_vmem = pl.BlockSpec(memory_space=vmem)
    in_hbm = pl.BlockSpec(memory_space=pltpu.HBM)
    return pl.pallas_call(
        functools.partial(experts_kernel, cuts),
        in_specs=[in_hbm] * 4 + [in_vmem] * 4 + [in_hbm],
        out_specs=[in_hbm] + [in_vmem] * 3 + [in_hbm] * 13,
        out_shape=[
            shape((RING * rows, width), bf16),
            shape((rows, width), bf16),
            shape((rows, width), f32),
            shape((EXPERTS + 8, width), f32),
            shape((locals_ // 2, 2, width, ff), f32),
            shape((locals_ // 2, width, ff), f32),
            shape((locals_, groups * CAP, width), bf16),
            shape((locals_, groups * CAP, width), bf16),
            shape((locals_, groups * CAP, 3 * ff), bf16),
            shape((RING, RING, RING, rows, cols), bf16),
            shape((locals_ // 2, 3, width, ff), bf16),
        ]
        + hbm_out,
        scratch_shapes=bufs
        + [
            vmem((rows, cols), bf16),
            vmem((rows, width), bf16),
            vmem((rows, width), bf16),
            dma((118,)),
            dma((118,)),
            dma((3, 4, 7)),
            dma((2, 2)),
            dma((5,)),
            dma((2,)),
            dma,
            dma((2, 3)),
            dma((2,)),
            dma((2,)),
        ],
        compiler_params=pltpu.CompilerParams(
            collective_id=collective_id, has_side_effects=True, vmem_limit_bytes=VMEM_LIMIT
        ),
        cost_estimate=pl.CostEstimate(flops=0, bytes_accessed=0, transcendentals=0),
        name="experts",
    )(x_all, dy_all, w_own, w_pair, resid, chances, router, ffn_norm, cot)


def reduce_plane_part(links, order, region, pair_in, bufs):
    pass_a, land_a, pass_b, land_b = bufs
    a1, a2 = order
    steps = (2, 1, -1, 0)
    given = []
    for i, step in enumerate(steps):
        places = {a1: links.rel(a1, step)}
        src = region(places, 1 - links.core)
        given.append(links.send(src, pair_in.at[i], links.pair()))
    yield
    mine = {}
    for i, step in enumerate(steps):
        mine[step] = region({a1: links.rel(a1, step)}, links.core)
        links.arrive(given[i], pair_in.at[i])
        add_into(mine[step], pair_in.at[i])
    yield from reduce_small(links, a1, lambda step: mine[step], mine[0], pass_a, land_a)
    yield

    def at(step):
        return region({a1: links.at[a1], a2: links.rel(a2, step)}, links.core)

    yield from reduce_small(links, a2, at, at(0), pass_b, land_b)


def plane_buffers(rows, size):
    return [
        pltpu.VMEM(shape, jnp.bfloat16)
        for shape in (
            (4, RING, rows, size),
            (2, RING, rows // 2, size),
            (2, RING, rows, size),
            (2, rows // 2, size),
            (2, rows, size),
        )
    ]


def back_kernel(
    lengths,
    d_resid,
    weights,
    heads,
    raw,
    stats,
    lse,
    mixed,
    normed,
    tokens,
    attn_norm,
    q_gain,
    k_gain,
    d_resid_mine,
    small_rows,
    out_mine,
    freqs,
    input_grad,
    out,
    grad_qkv,
    grad_out,
    grad_router,
    grad_attn,
    grad_ffn,
    grad_q,
    grad_k,
    terms,
    d_mixed,
    d_rot,
    d_proj,
    sums,
    sums_in,
    parts,
    passing,
    landing,
    d_normed,
    grads_in,
    rows_small,
    held,
    small_in,
    *rest,
):
    f32, bf16 = jnp.float32, jnp.bfloat16
    bufs, (send_sems, recv_sems, local_sem) = rest[:-3], rest[-3:]
    links = Links((X, Z, Y), send_sems, recv_sems, pair=True, extra=[(Y, 2), (X, 2), (Z, 2)])
    x, z, y = links.at
    core = links.core
    cols = q_gain.shape[1]
    rows, width = tokens.shape
    quarter = rows // RING
    block_rows = terms.shape[3]
    mine = pl.ds(pl.multiple_of(y * quarter, quarter), quarter)
    out_here = pltpu.make_async_copy(out_mine, out.at[mine], local_sem)
    out_here.start()

    def out_view(places, half):
        size = quarter if half is None else quarter // 2
        start = places[Y] * quarter + (half or 0) * size
        return out.at[pl.ds(pl.multiple_of(start, size), size)]

    out_sharing = gather_part(links, out_view, out_mine, (Y,))
    position, allowed = packed_layout(lengths)
    cosine, sine = rope_rows(position, freqs[...])
    scale = HEAD ** (-0.5)

    def weight(start, stop):
        return weights[:, :, :, :, start:stop].reshape(width, stop - start)

    d_mixed[...] = dot(d_resid[...], weight(3 * cols, 4 * cols), NN).astype(bf16)
    rows_small[...] = jnp.zeros(rows_small.shape, f32)
    rows_small[: small_rows.shape[0], :] = small_rows[...]
    means = [jnp.zeros((rows, 1), f32), jnp.zeros((rows, 1), f32)]
    for h in range(cols // HEAD):
        own = slice(h * HEAD, (h + 1) * HEAD)
        query, key, value = (
            heads[:, j * cols + h * HEAD : j * cols + (h + 1) * HEAD] for j in range(3)
        )
        scores = dot(query, key, NT) * scale
        probs = jnp.exp(jnp.where(allowed, scores, -1e30) - lse[:, h : h + 1])
        probs = jnp.where(allowed, probs, 0.0)
        d_out = d_mixed[:, own]
        d_proj[:, 2 * cols + h * HEAD : 2 * cols + (h + 1) * HEAD] = dot(
            probs.astype(bf16), d_out, TN
        ).astype(bf16)
        d_probs = dot(d_out, value, NT)
        d_scores = probs * (d_probs - jnp.sum(probs * d_probs, axis=-1, keepdims=True))
        d_scores = d_scores.astype(bf16)
        turned = (dot(d_scores, key, NN) * scale, dot(d_scores, query, TN) * scale)
        for j, (grad, gain) in enumerate(zip(turned, (q_gain, k_gain))):
            at = slice(j * cols + h * HEAD, j * cols + (h + 1) * HEAD)
            grad = grad * cosine - swap(grad) * sine
            hat = raw[:, at] * stats[:, j : j + 1]
            place_at = pl.ds(pl.multiple_of(y * cols + h * HEAD, HEAD), HEAD)
            rows_small[66 + j : 67 + j, place_at] = jnp.sum(grad * hat, axis=0, keepdims=True)
            grad = grad * gain[:, own]
            d_rot[:, at] = grad
            means[j] = means[j] + jnp.sum(grad * hat, axis=-1, keepdims=True)
    sent = start_sums(links, means, sums, sums_in)

    def fill(left, right, start):
        size = right.shape[1]

        @pl.loop(0, RING)
        def _(i):
            block = 2 * RING * block_rows
            some = left[:, pl.ds(pl.multiple_of(i * block, block), block)]
            terms[i, :, :, :, start : start + size] = (
                dot(some, right, TN).astype(bf16).reshape(RING, 2, block_rows, size)
            )

    def region(cut, places, at_core):
        index = tuple(places.get(axis, slice(None)) for axis in (X, Z))
        return terms.at[index + (at_core, slice(None), cut)]

    def reduction(part, start, size, order):
        own = bufs[5 * part : 5 * part + 5]
        cut = pl.ds(start, size)
        return reduce_plane_part(links, order, functools.partial(region, cut), own[0], own[1:])

    fill(normed, d_proj[:, 2 * cols :], 2 * cols)
    fill(d_resid, mixed[...], 3 * cols)
    first = reduction(0, 2 * cols, 2 * cols, (X, Z))
    next(first)
    total = end_sums(links, sent, sums, sums_in) / (HEADS * HEAD)
    for j in range(2):
        at = slice(j * cols, (j + 1) * cols)
        inverse = stats[:, j : j + 1]
        hat = raw[:, at] * inverse
        d_proj[:, at] = (inverse * (d_rot[:, at] - hat * total[:, j : j + 1])).astype(bf16)
    next(first)
    proj = weight(0, 3 * cols)

    def quarter_rows(step):
        return pl.ds(pl.multiple_of(links.rel(Y, step) * quarter, quarter), quarter)

    for k, step in enumerate((2, 1, -1)):
        parts[k] = dot(d_proj[quarter_rows(step), :], proj, NT).astype(bf16)
    by_step = {2: parts.at[0], 1: parts.at[1], -1: parts.at[2]}
    summing = reduce_small(links, Y, by_step.get, d_normed, passing, landing)
    next(summing)
    d_normed[...] = dot(d_proj[mine, :], proj, NT)
    fill(normed, d_proj[:, : 2 * cols], 0)
    second = reduction(1, 0, 2 * cols, (Z, X))
    next(second)
    next(summing)
    next(first)
    run_all([summing])
    hidden = tokens[mine, :].astype(f32)
    inverse = lax.rsqrt(jnp.mean(hidden * hidden, axis=-1, keepdims=True) + EPSILON)
    hat = hidden * inverse
    rows_small[64:65, :] = jnp.sum(d_normed[...] * hat, axis=0, keepdims=True)
    d_hat = d_normed[...] * attn_norm[...]
    final = d_resid_mine[...] + inverse * (
        d_hat - hat * jnp.mean(d_hat * hat, axis=-1, keepdims=True)
    )
    grads_in[y] = final.astype(bf16)

    def grads_view(places, half):
        if half is None:
            return grads_in.at[places[Y]]
        return grads_in.at[places[Y], pl.ds(half * (quarter // 2), quarter // 2)]

    sharing = gather_part(links, grads_view, grads_in.at[y], (Y,))
    next(sharing)
    next(out_sharing)
    wide = 4 * cols
    terms[:, :, :, :, wide:] = (
        rows_small[...].T.astype(bf16).reshape(RING, RING, 2, block_rows, rows_small.shape[0])
    )
    third = reduction(2, wide, rows_small.shape[0], (X, Z))
    next(third)
    next(second)
    next(first, None)
    next(second, None)
    run_all([third, first, second, sharing, out_sharing])

    here = terms.at[x, z, core]
    small = here.at[:, pl.ds(wide, rows_small.shape[0])]
    sent = [links.send(small, small_in.at[k], links.peer(Y, k + 1)) for k in range(3)]
    for j in range(3):
        grad_qkv[j] = here[:, j * cols : (j + 1) * cols].astype(f32)
    grad_out[...] = here[:, 3 * cols : 4 * cols].astype(f32)
    total = small[...].astype(f32)
    for k in range(3):
        links.arrive(sent[k], small_in.at[k])
        total = total + small_in[k].astype(f32)
    held[x, z, core] = total.astype(bf16)
    own = held.at[x, z, core]
    sent = [links.send(own, own, links.peer(X, step)) for step in (2, 1, -1)]
    for q in range(RING):
        input_grad[q * quarter : (q + 1) * quarter, :] = grads_in[q].astype(f32)
    for k, step in zip(sent, (2, 1, -1)):
        links.arrive(k, held.at[links.rel(X, -step), z, core])
    own = held.at[:, z, core]
    sent = [links.send(own, own, links.peer(Z, step)) for step in (2, 1, -1)]
    for k, step in zip(sent, (2, 1, -1)):
        links.arrive(k, held.at[:, links.rel(Z, -step), core])
    own = held.at[:, :, core]
    k = links.send(own, own, links.pair())
    links.arrive(k, held.at[:, :, 1 - core])
    total = held[...].astype(f32).reshape(width, rows_small.shape[0])
    grad_router[...] = total[:, :EXPERTS]
    rows_small[...] = total.T
    grad_attn[...] = rows_small[64:65, :]
    grad_ffn[...] = rows_small[65:66, :]
    out_here.wait()
    cut = pl.ds(pl.multiple_of(y * cols, cols), cols)
    grad_q[...] = rows_small[66:67, cut]
    grad_k[...] = rows_small[67:68, cut]
    links.close()


def back(
    lengths,
    d_resid,
    weights,
    heads,
    raw,
    stats,
    lse,
    mixed,
    normed,
    tokens,
    attn_norm,
    q_gain,
    k_gain,
    d_resid_mine,
    small_rows,
    out_mine,
    collective_id,
):
    bf16, f32 = jnp.bfloat16, jnp.float32
    rows, width = tokens.shape
    cols = q_gain.shape[1]
    quarter = rows // RING
    block_rows = weights.shape[3]
    half = HEAD // 2
    freqs = 10000.0 ** (-jnp.arange(half, dtype=f32) / half)
    freqs = jnp.concatenate([freqs, freqs])[None, :]
    in_vmem = pl.BlockSpec(memory_space=pltpu.VMEM)
    shape = jax.ShapeDtypeStruct
    vmem = pltpu.VMEM
    buffers = []
    for size in (2 * cols, 2 * cols, 128):
        buffers += plane_buffers(block_rows, size)
    return pl.pallas_call(
        back_kernel,
        in_specs=[pl.BlockSpec(memory_space=pltpu.SMEM)] + [in_vmem] * 16,
        out_specs=[in_vmem, pl.BlockSpec(memory_space=pltpu.HBM)] + [in_vmem] * 7,
        out_shape=[
            shape((rows, width), f32),
            shape((rows, width), bf16),
            shape((3, block_rows, cols), f32),
            shape((block_rows, cols), f32),
            shape((width, EXPERTS), f32),
            shape((1, width), f32),
            shape((1, width), f32),
            shape((1, cols), f32),
            shape((1, cols), f32),
        ],
        scratch_shapes=[
            vmem((RING, RING, 2, block_rows, 4 * cols + 128), bf16),
            vmem((rows, cols), bf16),
            vmem((rows, 2 * cols), f32),
            vmem((rows, 3 * cols), bf16),
            vmem((8, rows), f32),
            vmem((3, 8, rows), f32),
            vmem((3, quarter, width), bf16),
            vmem((2, quarter // 2, width), bf16),
            vmem((2, quarter, width), bf16),
            vmem((quarter, width), f32),
            vmem((RING, quarter, width), bf16),
            vmem((128, width), f32),
            vmem((RING, RING, 2, block_rows, 128), bf16),
            vmem((3, block_rows, 128), bf16),
        ]
        + buffers
        + [
            pltpu.SemaphoreType.DMA((80,)),
            pltpu.SemaphoreType.DMA((80,)),
            pltpu.SemaphoreType.DMA,
        ],
        compiler_params=pltpu.CompilerParams(
            collective_id=collective_id, has_side_effects=True, vmem_limit_bytes=VMEM_LIMIT
        ),
        cost_estimate=pl.CostEstimate(flops=0, bytes_accessed=0, transcendentals=0),
        name="back",
    )(
        lengths,
        d_resid,
        weights,
        heads,
        raw,
        stats,
        lse,
        mixed,
        normed,
        tokens,
        attn_norm,
        q_gain,
        k_gain,
        d_resid_mine,
        small_rows,
        out_mine,
        freqs,
    )


def body(
    tokens,
    attn_norm,
    qkv_weights,
    out_weight,
    q_gain,
    k_gain,
    ffn_norm,
    router,
    expert_weights,
    lengths,
    expert_ids,
    cotangent,
):
    blocks = jnp.concatenate([qkv_weights[0], qkv_weights[1], qkv_weights[2], out_weight], axis=1)
    pairs = [(i, i ^ 1) for i in range(lax.axis_size("expert"))]
    pair_weights = lax.ppermute(expert_weights, "expert", pairs)
    all_weights, rows_all, cot_rows, normed_b, heads, raw, inverses, lse, mixed_b, resid, chances = front(
        lengths,
        blocks,
        tokens,
        attn_norm[None],
        q_gain[None],
        k_gain[None],
        ffn_norm[None],
        router,
        expert_ids,
        cotangent,
        1,
    )
    d_resid, out_mine, d_resid_mine, small_rows, grad_experts, grad_down = experts(
        rows_all,
        cot_rows,
        expert_weights,
        pair_weights,
        resid,
        chances,
        router,
        ffn_norm[None],
        cotangent,
        3,
    )[:6]
    input_grad, output, grad_qkv, grad_out, grad_router, grad_attn, grad_ffn, grad_q, grad_k = back(
        lengths,
        d_resid,
        all_weights,
        heads,
        raw,
        inverses,
        lse,
        mixed_b,
        normed_b,
        tokens,
        attn_norm[None],
        q_gain[None],
        k_gain[None],
        d_resid_mine,
        small_rows,
        out_mine,
        4,
    )
    return (
        output,
        input_grad,
        grad_attn[0],
        grad_qkv,
        grad_out,
        grad_q[0],
        grad_k[0],
        grad_ffn[0],
        grad_router,
        grad_experts,
        grad_down,
    )


def solution(mesh):
    placed = (
        P(("dp", "expert"), None),
        P(),
        P(None, ("dp", "expert"), "mp"),
        P(("dp", "expert"), "mp"),
        P("mp"),
        P("mp"),
        P(),
        P(),
        P(("dp", "expert"), None, None, "mp"),
        P(("dp", "expert"), None),
        P(("dp", "expert"), None),
        P(("dp", "expert"), None),
    )
    return jax.shard_map(
        body,
        mesh=mesh,
        in_specs=placed,
        out_specs=(
            P(("dp", "expert"), None),
            P(("dp", "expert"), None),
            P(),
            P(None, ("dp", "expert"), "mp"),
            P(("dp", "expert"), "mp"),
            P("mp"),
            P("mp"),
            P(),
            P(),
            P(("dp", "expert"), None, None, "mp"),
            P(("dp", "expert"), None, "mp"),
        ),
        check_vma=False,
    )
```

time: 1690 us -> 507 us (0.30)
  the two profiles are of different devices: /device:TPU:0 before, /device:TPU:1 now
where the time goes in v1:
time: 507 us; the launch traced here: 499 us
  Pallas kernels  468 us (92%)
  local copies, waits for them, and re-layouts  25.5 us (5%)
    pallas_call x1, Pallas kernels, experts(): pl.pallas_call(functools.partial(experts_kernel, cuts), in_specs=[in_hbm]...  196 us
    pallas_call x1, Pallas kernels, front(): pl.pallas_call(functools.partial(front_kernel, cut_as(4, 6, 7), cut_as(4,...  179 us
    pallas_call x1, Pallas kernels, back(): pl.pallas_call(back_kernel, in_specs=[pl.BlockSpec(memory_space=pltpu.SME...  93.3 us
    unnamed x27, local copies, waits for them, and re-layouts  24.6 us
  transfers between devices with their start and end apart: 1, of which 0 were waited for; matrix products, arithmetic and copies ran while one was open for 1% of the time, Pallas kernels for 36%

profile of v1, /device:TPU:1, one launch (start us, length us, event | category | flops | bytes accessed | tf_op | source)
XLA Modules:
  0.0 498.6 jit_solution(9285752772411153383)
XLA Ops:
  0.6 1.5 collective-permute-start
  2.1 1.5 copy.24.ids
  3.6 2.0 copy.23.router
  5.6 0.6 maximum_bitcast_fusion.freqs
  6.2 0.9 slice_bitcast_fusion.2
  7.1 1.6 pad_maximum_fusion.blocks
  8.7 178.6 %front.1 = (bf16[4,4,2,64,2048]{4,3,2,1,0:T(8,128)(2,1)}, bf16[4,4,4,64,2176]{4,3,2,1,0:T(8,128)(2,1)}, bf16[4,4,4,64,2048]{4,3,2,1,0:T(8,128)(2,1)}, bf16[256,2...) custom-call(s32[1,4]{1,0:T(1,128)} %lengths.3, ...), custom_call_target="tpu_custom_call" | custom-call | tf_op jit(solution)/shard_map/front/pallas_call | solution.py:509
  187.3 0.0 collective-permute-done.w_pair
  187.3 196.3 %experts.1 = (bf16[256,2048]{1,0:T(8,128)(2,1)}, bf16[64,2048]{1,0:T(8,128)(2,1)}, f32[64,2048]{1,0:T(8,128)}, f32[72,2048]{1,0:T(8,128)}, f32[2,2,2048,256]{3,2...) custom-call(bf16[4,4,4,64,2176]{4,3,2,1,0:T(8,128)(2,1)} %get-tuple-, ...), custom_call_target="tpu_custom_call" | custom-call | tf_op jit(solution)/shard_map/experts/pallas_call | solution.py:1273
  383.7 93.3 %back.1 = (f32[256,2048]{1,0:T(8,128)}, bf16[256,2048]{1,0:T(8,128)(2,1)}, f32[3,64,512]{2,1,0:T(8,128)}, f32[64,512]{1,0:T(8,128)}, f32[2048,64]{1,0:T(8,128)},...) custom-call(s32[1,4]{1,0:T(1,128)} %lengths.3, ...), custom_call_target="tpu_custom_call" | custom-call | tf_op jit(solution)/shard_map/back/pallas_call | solution.py:1598
  477.0 0.0 copy-start.4
  477.0 0.0 copy-start.1
  477.0 0.0 copy-start.2
  477.1 2.4 copy.26
  479.4 2.3 copy.37
  481.7 3.1 copy.38
  484.9 0.6 copy.39
  485.5 0.7 copy.40
  486.2 0.7 copy.41
  486.9 0.6 copy.42
  487.5 0.6 copy.43
  488.1 0.6 copy.44
  488.7 7.5 %copy.45 = f32[2,2,2048,256]{3,2,1,0:T(8,128)} copy(f32[2,2,2048,256]{3,2,1,0:T(8,128)} %get-tuple-element.97) | data formatting | bytes 16777216
  496.2 2.0 copy.46
  (12 shorter events, 0.0 us)
Async XLA Ops:
  0.6 186.6 %collective-permute-start = (bf16[2,3,2048,256]{3,2,1,0:T(8,128)(2,1)}, bf16[2,3,2048,256]{3,2,1,0:T(8,128)(2,1)}, u32[]{:S(2)}, u32[]{:S(2)}) collective-permute-start(bf16[2,3,2048,256]{3,2,1,0:T(8,128)(2,1)} %w_own.1), channel_id=1, source_target_pairs={{0,4},{4,0},{8,12},{12,8},{16,20},{20,16},{24,28},{28,24},{1,5},{5... | collective-permute-start | bytes 18874376 | tf_op jit(solution)/shard_map/ppermute | solution.py:1677
  477.0 7.9 %copy-start.4 = (f32[1,2048]{1,0:T(1,128)S(1)}, f32[1,2048]{1,0:T(1,128)}, u32[]{:S(2)}) copy-start(f32[1,2048]{1,0:T(1,128)} %get-tuple-element.54) | copy-start | bytes 24580
  477.0 8.5 %copy-start.1 = (f32[3,64,512]{2,1,0:T(8,128)S(1)}, f32[3,64,512]{2,1,0:T(8,128)}, u32[]{:S(2)}) copy-start(f32[3,64,512]{2,1,0:T(8,128)} %get-tuple-element.91) | copy-start | bytes 1179652
  477.0 9.2 %copy-start.2 = (f32[64,512]{1,0:T(8,128)S(1)}, f32[64,512]{1,0:T(8,128)}, u32[]{:S(2)}) copy-start(f32[64,512]{1,0:T(8,128)} %get-tuple-element.92) | copy-start | bytes 393220
  477.0 9.9 %copy-start.6 = (f32[1,512]{1,0:T(1,128)S(1)}, f32[1,512]{1,0:T(1,128)}, u32[]{:S(2)}) copy-start(f32[1,512]{1,0:T(1,128)} %get-tuple-element.57) | copy-start | bytes 6148
  477.0 10.4 %copy-start.5 = (f32[1,512]{1,0:T(1,128)S(1)}, f32[1,512]{1,0:T(1,128)}, u32[]{:S(2)}) copy-start(f32[1,512]{1,0:T(1,128)} %get-tuple-element.58) | copy-start | bytes 6148
  477.0 11.0 %copy-start.3 = (f32[1,2048]{1,0:T(1,128)S(1)}, f32[1,2048]{1,0:T(1,128)}, u32[]{:S(2)}) copy-start(f32[1,2048]{1,0:T(1,128)} %get-tuple-element.59) | copy-start | bytes 24580
  488.7 7.5 %copy-start = (f32[2,2048,256]{2,1,0:T(8,128)S(1)}, f32[2,2048,256]{2,1,0:T(8,128)}, u32[]{:S(2)}) copy-start(f32[2,2048,256]{2,1,0:T(8,128)} %get-tuple-element.98) | copy-start | bytes 12582916

commit v2 on v1

--- a/solution.py
+++ b/solution.py
@@ -13,7 +13,7 @@
 SEQS = 4
 EXPERTS = 64
 CAP = 48
-VMEM_LIMIT = 60 * 1024 * 1024
+VMEM_LIMIT = 63000000
 
 
 EPSILON = 1e-05
@@ -291,11 +291,31 @@
     return jnp.concatenate([total, fill], axis=0).T
 
 
+FRONT = (
+    (
+        0, 1, 2, 3, 1, 3, 0, 1, 4, 0, 1, 1, 0, 0, 2, 4, 3, 1, 3, 4, 2, 0, 2, 3, 2, 4, 4,
+    ),
+    (
+        4, 3, 4, 3,
+    ),
+    (),
+    (),
+    (),
+    (),
+    (),
+    (
+        6, 7, 4, 4, 5, 7, 3, 6, 2, 7, 5, 5, 6, 3, 2, 7, 7, 4, 7, 6, 6, 6, 5, 3, 7, 6, 2,
+        2, 5, 5, 7, 7, 2, 5, 6, 6, 5, 5, 7, 6, 5,
+    ),
+)
+
+
 def front_kernel(
     cuts,
     cot_cuts,
     lengths,
-    blocks,
+    qkv,
+    out_weight,
     tokens,
     attn_norm,
     q_gain,
@@ -323,12 +343,28 @@
     passing,
     landing,
     shard,
+    chosen,
+    blocks,
+    whole,
     send_sems,
     recv_sems,
     local_sems,
 ):
     f32, bf16 = jnp.float32, jnp.bfloat16
+    cols = q_gain.shape[1]
+    pieces = [
+        pltpu.make_async_copy(
+            qkv.at[j] if j < 3 else out_weight,
+            blocks.at[:, pl.ds(j * cols, cols)],
+            local_sems.at[3 + j],
+        )
+        for j in range(4)
+    ]
+    for piece in pieces:
+        piece.start()
     links = Links((X, Z, Y), send_sems, recv_sems, pair=True, extra=[(Y, 2)])
+    for piece in pieces:
+        piece.wait()
     x, z, y = links.at
     core = links.core
     own_block = pltpu.make_async_copy(blocks, weights.at[x, z, core], local_sems.at[0])
@@ -384,25 +420,31 @@
     cot_gathers = row_gathers(cot_out, cot_mine, cot_cuts, (X, Z, Y))
     for gather in cot_gathers:
         next(gather)
+    parts_of = gathers + cot_gathers
+
+    def steps(segment):
+        for part in FRONT[segment]:
+            next(parts_of[part], None)
+
     hidden = tokens[...].astype(f32)
     attn_inv = lax.rsqrt(jnp.mean(hidden * hidden, axis=-1, keepdims=True) + EPSILON)
     normed[...] = (hidden * attn_inv * attn_norm[...]).astype(bf16)
     position, allowed = packed_layout(lengths)
     cosine, sine = rope_rows(position, freqs[...])
+    expert = lax.broadcasted_iota(jnp.int32, (128, TOK), 0)
+    picks = jnp.zeros((128, TOK), f32)
+    for k in range(ids.shape[0]):
+        picks = picks + jnp.where(ids[k : k + 1, :] == expert, 1.0, 0.0)
+    chosen[...] = picks.T
     cot_here.wait()
-    for _ in range(6):
-        for gather in gathers + cot_gathers:
-            next(gather, None)
+    steps(0)
     run_all(gathers)
     for k, dst in given:
         links.arrive(k, dst)
     own_block.wait()
-    for gather in cot_gathers[1:]:
-        next(gather)
     save = pltpu.make_async_copy(weights, all_weights, local_sems.at[0])
     save.start()
 
-    cols = q_gain.shape[1]
     width = tokens.shape[1]
 
     def project(j):
@@ -416,6 +458,7 @@
         squares.append(jnp.sum(value * value, axis=-1, keepdims=True))
     sent = start_sums(links, squares, sums, sums_in)
     heads[:, 2 * cols :] = project(2).astype(bf16)
+    steps(1)
     total = end_sums(links, sent, sums, sums_in)
     inverse = lax.rsqrt(total / (HEADS * HEAD) + EPSILON)
     stats[...] = inverse
@@ -429,6 +472,7 @@
             part = (part * cosine + swap(part) * sine).astype(bf16)
             heads[:, j * cols + h * HEAD : j * cols + (h + 1) * HEAD] = part
             rotated.append(part)
+        steps(2 + h)
         scores = dot(rotated[0], rotated[1], NT) * HEAD ** (-0.5)
         scores = jnp.where(allowed, scores, -1e30)
         top = jnp.max(scores, axis=-1, keepdims=True)
@@ -438,31 +482,28 @@
         value = heads[:, 2 * cols + h * HEAD : 2 * cols + (h + 1) * HEAD]
         mixed[:, own] = dot(probs, value, NN).astype(bf16)
     lse[...] = lanes_of(top_sums, TOK)
-
+    steps(6)
     out_w = weights[:, :, :, :, 3 * cols :].reshape(width, cols)
     def quarter_rows(step):
         return pl.ds(pl.multiple_of(links.rel(Y, step) * quarter, quarter), quarter)
 
+    whole[...] = dot(mixed[...], out_w, NT)
     for k, step in enumerate((2, 1, -1)):
-        parts[k] = dot(mixed[quarter_rows(step), :], out_w, NT).astype(bf16)
+        parts[k] = whole[quarter_rows(step), :].astype(bf16)
     by_step = {2: parts.at[0], 1: parts.at[1], -1: parts.at[2]}
     summing = reduce_small(links, Y, by_step.get, resid, passing, landing)
     next(summing)
     rows = quarter_rows(0)
-    resid[...] = tokens[rows, :].astype(f32) + dot(mixed[rows, :], out_w, NT)
+    resid[...] = tokens[rows, :].astype(f32) + whole[rows, :]
     run_all([summing])
     total = resid[...]
     ffn_inv = lax.rsqrt(jnp.mean(total * total, axis=-1, keepdims=True) + EPSILON)
     moe_in = (total * ffn_inv * ffn_norm[...]).astype(bf16)
-    logits = dot(moe_in, router[...], NN)
+    logits = dot(moe_in, router[...], NT)
     logits = logits - jnp.max(logits, axis=-1, keepdims=True)
     chances = jnp.exp(logits)
     chances = chances / jnp.sum(chances, axis=-1, keepdims=True)
-    mine = ids[rows, :]
-    expert = lax.broadcasted_iota(jnp.int32, chances.shape, 1)
-    picks = jnp.zeros(chances.shape, f32)
-    for k in range(ids.shape[1]):
-        picks = picks + jnp.where(mine[:, k : k + 1] == expert, 1.0, 0.0)
+    picks = chosen[rows, :EXPERTS]
     both = jnp.concatenate([chances, picks], axis=1)
     probs_out[...] = both
     shard[:, :width] = moe_in
@@ -470,34 +511,37 @@
     here = pltpu.make_async_copy(shard, rows_out.at[x, z, y], local_sems.at[1])
     here.start()
 
-    gathers = row_gathers(rows_out, shard, cuts, ())
-    last_y, others = cot_gathers[0], cot_gathers[1:]
-
-    def step(parts, count=1):
-        for _ in range(count):
-            for part in parts:
-                next(part, None)
-
-    step(gathers)
-    here.wait()
-    step(others, 2)
-    step([last_y])
-    step(gathers, 6)
-    step(others)
-    step([last_y], 2)
-    step(gathers, 2)
-    run_all([last_y] + others + gathers)
+    parts_of += row_gathers(rows_out, shard, cuts, ())
+    seen = set()
+    for part in FRONT[7]:
+        if part >= 5 and part in seen and here is not None:
+            here.wait()
+            here = None
+        seen.add(part)
+        next(parts_of[part], None)
+    run_all(parts_of)
     save.wait()
     links.close()
 
 
 def front(
-    lengths, blocks, tokens, attn_norm, q_gain, k_gain, ffn_norm, router, ids, cot, collective_id
+    lengths,
+    qkv,
+    out_weight,
+    tokens,
+    attn_norm,
+    q_gain,
+    k_gain,
+    ffn_norm,
+    router,
+    ids,
+    cot,
+    collective_id,
 ):
     bf16, f32 = jnp.bfloat16, jnp.float32
-    block_rows, wide = blocks.shape
     rows, width = tokens.shape
     cols = q_gain.shape[1]
+    block_rows, wide = out_weight.shape[0], 4 * cols
     quarter = rows // RING
     ext = width + 128
     half = HEAD // 2
@@ -508,7 +552,7 @@
     shape = jax.ShapeDtypeStruct
     return pl.pallas_call(
         functools.partial(front_kernel, cut_as(4, 6, 7), cut_as(4, 6, 6)),
-        in_specs=[pl.BlockSpec(memory_space=pltpu.SMEM), in_hbm] + [in_vmem] * 8 + [in_hbm],
+        in_specs=[pl.BlockSpec(memory_space=pltpu.SMEM)] + [in_hbm] * 2 + [in_vmem] * 8 + [in_hbm],
         out_specs=[in_hbm, in_hbm, in_hbm] + [in_vmem] * 8,
         out_shape=[
             shape((RING, RING, 2, block_rows, wide), bf16),
@@ -531,16 +575,32 @@
             pltpu.VMEM((2, quarter // 2, width), bf16),
             pltpu.VMEM((2, quarter, width), bf16),
             pltpu.VMEM((quarter, ext), bf16),
+            pltpu.VMEM((rows, 128), f32),
+            pltpu.VMEM((block_rows, wide), bf16),
+            pltpu.VMEM((rows, width), f32),
             pltpu.SemaphoreType.DMA((282,)),
             pltpu.SemaphoreType.DMA((282,)),
-            pltpu.SemaphoreType.DMA((3,)),
+            pltpu.SemaphoreType.DMA((7,)),
         ],
         compiler_params=pltpu.CompilerParams(
             collective_id=collective_id, has_side_effects=True, vmem_limit_bytes=VMEM_LIMIT
         ),
         cost_estimate=pl.CostEstimate(flops=0, bytes_accessed=0, transcendentals=0),
         name="front",
-    )(lengths, blocks, tokens, attn_norm, q_gain, k_gain, ffn_norm, router, ids, freqs, cot)
+    )(
+        lengths,
+        qkv,
+        out_weight,
+        tokens,
+        attn_norm,
+        q_gain,
+        k_gain,
+        ffn_norm,
+        router,
+        ids,
+        freqs,
+        cot,
+    )
 
 
 ORDER = (2, 1, -1, 0)
@@ -549,177 +609,166 @@
 def far_first(i):
     return 2 - i + 3 * (i * (i - 1) // 2)
 
+
+ORDERS = ((0, 1, 2), (1, 0, 2), (2, 0, 1))
+
+TILES = (9, 12, 12)
 
 PLAN = {
     (1, 0): (
         (0, 0, 0, 0, 0),
         (0, 1, 0, 0, 0),
+        (0, 2, 0, 0, 0),
         (0, 0, 1, 0, 0),
-        (0, 1, 0, 1, 0),
-    ),
-    (2, 0): (
-        (0, 2, 0, 0, 0),
         (0, 0, 2, 0, 0),
         (0, 0, 3, 0, 0),
+        (0, 1, 0, 1, 0),
         (0, 1, 0, 1, 1),
         (0, 2, 0, 1, 0),
         (0, 2, 0, 1, 1),
     ),
-    (2, 1): (
+    (2, 0): (
         (0, 1, 0, 2, 0),
         (0, 1, 0, 2, 1),
-    ),
-    (3, 0): (
-        (0, 1, 0, 3, 0),
-        (0, 1, 0, 3, 1),
+        (0, 2, 0, 2, 0),
+        (0, 2, 0, 2, 1),
         (0, 1, 1, 0, 0),
+        (0, 2, 1, 0, 0),
         (0, 0, 0, 1, 0),
         (0, 0, 0, 2, 0),
-        (0, 2, 0, 2, 0),
-        (0, 2, 0, 2, 1),
         (0, 0, 1, 1, 0),
         (0, 0, 1, 2, 0),
         (0, 1, 1, 1, 0),
-    ),
-    (3, 1): (
-        (0, 0, 0, 3, 0),
-        (0, 2, 0, 3, 0),
-        (0, 2, 0, 3, 1),
-        (0, 0, 1, 3, 0),
-    ),
-    (4, 0): (
-        (0, 1, 0, 4, 0),
-        (0, 2, 1, 0, 0),
         (0, 1, 1, 1, 1),
         (0, 2, 1, 1, 0),
         (0, 2, 1, 1, 1),
         (0, 0, 2, 1, 0),
         (0, 0, 3, 1, 0),
     ),
-    (4, 1): (
-        (0, 1, 0, 5, 0),
-        (1, 1, 0, 0, 0),
-        (0, 2, 0, 4, 0),
-        (0, 1, 1, 2, 0),
-        (0, 1, 1, 2, 1),
+    (2, 1): (
+        (0, 1, 0, 3, 0),
+        (0, 0, 0, 3, 0),
+        (0, 1, 0, 3, 1),
+        (0, 2, 0, 3, 0),
+        (0, 2, 0, 3, 1),
+        (0, 0, 1, 3, 0),
     ),
-    (5, 0): (
-        (0, 2, 0, 5, 0),
-        (1, 2, 0, 0, 0),
-        (0, 2, 1, 2, 0),
-        (0, 2, 1, 2, 1),
-        (0, 0, 2, 2, 0),
-        (0, 1, 1, 3, 0),
-        (0, 0, 3, 2, 0),
-        (0, 1, 1, 3, 1),
+    (3, 0): (
         (0, 1, 2, 0, 0),
+        (0, 2, 2, 0, 0),
         (0, 0, 0, 1, 1),
         (0, 0, 0, 2, 1),
         (0, 0, 1, 1, 1),
         (0, 0, 1, 2, 1),
+        (0, 0, 2, 1, 1),
         (0, 1, 2, 1, 0),
-    ),
-    (5, 1): (
-        (0, 0, 0, 3, 1),
-        (0, 0, 1, 3, 1),
-        (0, 2, 1, 3, 0),
-        (0, 2, 1, 3, 1),
-        (0, 0, 2, 3, 0),
-        (0, 0, 3, 3, 0),
-    ),
-    (6, 0): (
-        (0, 1, 1, 4, 0),
-        (0, 2, 2, 0, 0),
-        (0, 0, 2, 1, 1),
         (0, 1, 2, 1, 1),
         (0, 2, 2, 1, 0),
         (0, 2, 2, 1, 1),
         (0, 0, 3, 1, 1),
     ),
-    (6, 1): (
-        (0, 1, 1, 5, 0),
-        (0, 2, 1, 4, 0),
-        (1, 1, 0, 3, 0),
-        (0, 1, 2, 2, 0),
-        (0, 1, 2, 2, 1),
+    (3, 2): (
+        (0, 1, 0, 4, 0),
+        (0, 2, 0, 4, 0),
+        (0, 1, 1, 2, 0),
+        (0, 1, 1, 2, 1),
+        (0, 2, 1, 2, 0),
+        (0, 2, 1, 2, 1),
+        (0, 0, 0, 3, 1),
+        (0, 0, 1, 3, 1),
     ),
-    (7, 0): (
-        (0, 2, 1, 5, 0),
-        (1, 2, 0, 3, 0),
-        (0, 0, 0, 4, 0),
-        (0, 0, 2, 2, 1),
-        (0, 2, 2, 2, 0),
-        (0, 2, 2, 2, 1),
-        (0, 1, 2, 3, 0),
-        (0, 1, 2, 3, 1),
+    (4, 0): (
+        (0, 1, 0, 5, 0),
+        (1, 1, 0, 0, 0),
+        (0, 2, 0, 5, 0),
+        (1, 2, 0, 0, 0),
+        (0, 0, 2, 2, 0),
+        (0, 1, 1, 3, 0),
+        (0, 1, 1, 3, 1),
+        (0, 2, 1, 3, 0),
+        (0, 2, 1, 3, 1),
         (0, 1, 3, 0, 0),
+        (0, 2, 3, 0, 0),
         (0, 1, 3, 1, 0),
-    ),
-    (7, 1): (
-        (0, 0, 0, 5, 0),
-        (1, 0, 0, 0, 0),
-        (0, 0, 1, 4, 0),
-        (0, 0, 3, 2, 1),
-        (0, 0, 2, 3, 1),
-        (0, 2, 2, 3, 0),
-        (0, 2, 2, 3, 1),
-    ),
-    (8, 0): (
-        (0, 0, 1, 5, 0),
-        (0, 1, 2, 4, 0),
-        (0, 0, 3, 3, 1),
-        (0, 2, 3, 0, 0),
         (0, 1, 3, 1, 1),
         (0, 2, 3, 1, 0),
         (0, 2, 3, 1, 1),
+        (0, 0, 3, 2, 0),
+        (0, 0, 2, 3, 0),
+        (0, 0, 3, 3, 0),
+        (3, 0, 0, 0, 0),
+        (0, 1, 2, 2, 0),
+        (0, 1, 2, 2, 1),
+        (0, 2, 2, 2, 0),
+        (0, 0, 2, 2, 1),
+        (0, 1, 2, 3, 0),
+        (0, 2, 2, 2, 1),
+        (0, 1, 1, 4, 0),
+        (0, 1, 2, 3, 1),
+        (0, 0, 0, 4, 0),
+        (0, 2, 2, 3, 0),
+        (0, 2, 1, 4, 0),
+        (0, 0, 2, 3, 1),
+        (0, 2, 2, 3, 1),
+        (0, 1, 1, 5, 0),
+        (1, 1, 0, 3, 0),
+        (0, 0, 0, 5, 0),
+        (1, 0, 0, 0, 0),
+        (0, 2, 1, 5, 0),
+        (0, 0, 1, 4, 0),
+        (0, 0, 3, 2, 1),
+        (1, 2, 0, 3, 0),
+        (0, 0, 1, 5, 0),
+        (0, 0, 3, 3, 1),
+        (3, 0, 0, 0, 0),
+        (3, 0, 0, 0, 0),
+        (3, 0, 0, 0, 0),
+        (3, 0, 0, 0, 0),
+        (0, 1, 3, 2, 0),
+        (0, 1, 3, 2, 1),
+        (0, 2, 3, 2, 0),
+        (0, 2, 3, 2, 1),
+        (0, 1, 3, 3, 0),
+        (0, 1, 2, 4, 0),
+        (0, 1, 3, 3, 1),
+        (0, 2, 3, 3, 0),
+        (0, 2, 2, 4, 0),
+        (0, 2, 3, 3, 1),
         (0, 1, 2, 5, 0),
         (1, 1, 0, 3, 1),
-        (0, 1, 3, 2, 0),
-        (0, 1, 3, 2, 1),
-        (0, 2, 2, 4, 0),
-        (0, 1, 3, 3, 0),
-        (0, 1, 3, 3, 1),
         (0, 0, 2, 4, 0),
         (0, 2, 2, 5, 0),
+        (1, 0, 0, 3, 0),
         (1, 2, 0, 3, 1),
         (0, 0, 2, 5, 0),
         (1, 0, 0, 3, 1),
-        (3, 0, 0, 0, 0),
         (0, 0, 3, 4, 0),
-        (0, 2, 3, 2, 0),
-        (0, 2, 3, 2, 1),
         (3, 0, 0, 0, 0),
         (0, 0, 3, 5, 0),
-        (0, 2, 3, 3, 0),
-        (0, 2, 3, 3, 1),
-        (1, 0, 0, 3, 0),
+        (0, 2, 3, 4, 0),
+        (0, 1, 3, 4, 0),
+        (0, 2, 3, 5, 0),
+        (0, 1, 3, 5, 0),
         (3, 0, 0, 0, 0),
         (3, 0, 0, 0, 0),
-        (0, 1, 3, 4, 0),
         (3, 0, 0, 0, 0),
-        (0, 1, 3, 5, 0),
+        (1, 0, 0, 5, 0),
+        (2, 0, 0, 0, 0),
         (1, 1, 0, 5, 0),
         (2, 1, 0, 0, 0),
         (3, 0, 0, 0, 0),
-        (0, 2, 3, 4, 0),
+        (2, 0, 0, 3, 0),
+        (2, 0, 0, 3, 1),
         (2, 1, 0, 3, 0),
         (2, 1, 0, 3, 1),
-        (0, 2, 3, 5, 0),
-        (1, 0, 0, 5, 0),
-        (2, 0, 0, 0, 0),
+        (3, 0, 0, 0, 0),
+        (2, 0, 0, 5, 0),
         (3, 0, 0, 0, 0),
         (2, 1, 0, 5, 0),
-        (2, 0, 0, 3, 0),
-        (2, 0, 0, 3, 1),
-        (3, 0, 0, 0, 0),
         (1, 2, 0, 5, 0),
         (2, 2, 0, 0, 0),
-        (2, 0, 0, 5, 0),
-        (3, 0, 0, 0, 0),
         (2, 2, 0, 3, 0),
         (2, 2, 0, 3, 1),
-        (3, 0, 0, 0, 0),
-        (3, 0, 0, 0, 0),
         (2, 2, 0, 5, 0),
     ),
 }
@@ -836,80 +885,18 @@
         add_into(self.acc(0), self.landing.at[0], self.landing.at[1])
 
 
-def experts_kernel(
-    cuts,
-    x_all,
-    dy_all,
-    w_own,
-    w_pair,
-    resid,
-    chances,
-    router,
-    ffn_norm,
-    cot,
-    d_resid,
-    out_mine,
-    d_resid_mine,
-    small_rows,
-    grad_experts,
-    grad_down,
-    xs,
-    ds,
-    act,
-    ret,
-    pair_in,
-    *refs,
-):
-    f32, bf16 = jnp.float32, jnp.bfloat16
-    hbm, refs = refs[:6], refs[6:]
-    bufs, refs = refs[:27], refs[27:]
-    (
-        home,
-        stage,
-        cot_now,
-        send_sems,
-        recv_sems,
-        ring_sems,
-        load_sems,
-        store_sems,
-        weight_sems,
-        cot_sem,
-        grad_load_sems,
-        grad_pair_sems,
-        grad_store_sems,
-    ) = refs
-    links = Links((X, Z, Y), send_sems, recv_sems, pair=True)
-    here_x, here_z, here_y = links.at
-    rows = ret.shape[3]
-    width = resid.shape[1]
-    ff = act.shape[2] // 3
-    cap = CAP
-    locals_ = xs.shape[0]
-    half_experts = locals_ // 2
-    group = (here_x * RING + here_z) * 2
-    ids = [(group + links.core) * half_experts + j for j in range(half_experts)]
-    ids += [(group + 1 - links.core) * half_experts + j for j in range(half_experts)]
-
-    cot_rows = cot.at[pl.ds(pl.multiple_of(here_y * rows, rows), rows)]
-    cot_load = pltpu.make_async_copy(cot_rows, cot_now, cot_sem)
-    cot_load.start()
-
-    def group_at(s, g):
-        gx = lax.rem(here_x + far_first(s // 2) + RING, RING)
-        gz = lax.rem(here_z + far_first(2 * (s % 2) + g) + RING, RING)
-        return gx, gz
-
-    orders = ((X, Z, Y), (Z, X, Y), (Y, X, Z))
+def ring_sums(links, source, cuts, orders, hbm, bufs, ring_sems):
+    rows = source.shape[3]
     far, near, last = [], [], []
     for p, ((start, size), (a1, a2, a3)) in enumerate(zip(cuts, orders)):
-        side, stg, acc, final, pass_b, land_b, pass_c, land_c, _ = bufs[9 * p : 9 * p + 9]
+        side, stg, acc, final, pass_b, land_b, pass_c, land_c = bufs[8 * p : 8 * p + 8]
         passed, landed = hbm[2 * p : 2 * p + 2]
 
         def term(a1, a2, c, start, size, step, half):
             places = {a1: links.rel(a1, step), a2: links.rel(a2, ORDER[c])}
             index = tuple(places.get(axis, slice(None)) for axis in (X, Z, Y))
             cut = slice(None) if half is None else pl.ds(half * (rows // 2), rows // 2)
-            return ret.at[index + (cut, pl.ds(start, size))]
+            return source.at[index + (cut, pl.ds(start, size))]
 
         slots = side.shape[0]
         chunks = []
@@ -942,18 +929,113 @@
                 land_c,
             )
         )
-
-    rings = (far, near, last)
+    return far, near, last
+
+
+def act_on(rings, actions, work=None):
+    for kind, p, c, method, d in actions:
+        if kind == 3:
+            next(work, None)
+            continue
+        ring = rings[0][p][c] if kind == 0 else rings[kind][p]
+        name = ("first", "direct", "prepare", "onward", "collect", "finish")[method]
+        call = getattr(ring, name)
+        call(d) if method in (1, 2, 3) else call()
+
+
+def ring_buffers(rows, cuts):
+    bf16, vmem = jnp.bfloat16, pltpu.VMEM
+    landing, buffers = [], []
+    for p, (_, size) in enumerate(cuts):
+        slots = 2 if p == 0 else 1
+        landing += [
+            jax.ShapeDtypeStruct((2, 4, RING, rows // 2, size), bf16),
+            jax.ShapeDtypeStruct((2, 4, RING, rows, size), bf16),
+        ]
+        buffers += [
+            vmem((slots, 2, RING, rows // 2, size), bf16),
+            vmem((slots, 2, RING, rows // 2, size), bf16),
+            vmem((4, RING, rows, size), bf16),
+            vmem((2, RING, rows, size), bf16),
+            vmem((2, RING, rows // 2, size), bf16),
+            vmem((2, RING, rows, size), bf16),
+            vmem((2, rows // 2, size), bf16),
+            vmem((2, rows, size), bf16),
+        ]
+    return landing, buffers
+
+
+def experts_kernel(
+    cuts,
+    x_all,
+    dy_all,
+    w_own,
+    w_pair,
+    resid,
+    chances,
+    router,
+    ffn_norm,
+    cot,
+    d_resid,
+    out_mine,
+    d_resid_mine,
+    small_rows,
+    grad_experts,
+    grad_down,
+    xs,
+    ds,
+    act,
+    ret,
+    pair_in,
+    *refs,
+):
+    f32, bf16 = jnp.float32, jnp.bfloat16
+    hbm, refs = refs[:6], refs[6:]
+    bufs, refs = refs[:24], refs[24:]
+    (
+        home,
+        stage,
+        cot_now,
+        send_sems,
+        recv_sems,
+        ring_sems,
+        load_sems,
+        store_sems,
+        weight_sems,
+        cot_sem,
+        grad_load_sems,
+        grad_pair_sems,
+        grad_store_sems,
+    ) = refs
+    links = Links((X, Z, Y), send_sems, recv_sems, pair=True)
+    here_x, here_z, here_y = links.at
+    rows = ret.shape[3]
+    width = resid.shape[1]
+    ff = act.shape[2] // 3
+    cap = CAP
+    locals_ = xs.shape[0]
+    half_experts = locals_ // 2
+    group = (here_x * RING + here_z) * 2
+    ids = [(group + links.core) * half_experts + j for j in range(half_experts)]
+    ids += [(group + 1 - links.core) * half_experts + j for j in range(half_experts)]
+
+    cot_rows = cot.at[pl.ds(pl.multiple_of(here_y * rows, rows), rows)]
+    cot_load = pltpu.make_async_copy(cot_rows, cot_now, cot_sem)
+    cot_load.start()
+
+    def group_at(s, g):
+        gx = lax.rem(here_x + far_first(s) + RING, RING)
+        gz = lax.rem(here_z + far_first(g) + RING, RING)
+        return gx, gz
+
+    rings = ring_sums(links, ret, cuts, ORDERS, hbm, bufs, ring_sems)
 
     def act_at(key, work=None):
-        for kind, p, c, method, d in PLAN.get(key, ()):
-            if kind == 3:
-                next(work, None)
-                continue
-            ring = far[p][c] if kind == 0 else rings[kind][p]
-            name = ("first", "direct", "prepare", "onward", "collect", "finish")[method]
-            call = getattr(ring, name)
-            call(d) if method in (1, 2, 3) else call()
+        act_on(rings, PLAN[key], work)
+
+    def bring_home():
+        for p, (start, size) in enumerate(cuts):
+            home[:, start : start + size] = bufs[8 * p + 2][3, links.at[ORDERS[p][2]]]
 
     lane = lax.broadcasted_iota(jnp.int32, (2 * locals_, 128), 1)
     row = lax.broadcasted_iota(jnp.int32, (2 * locals_, 128), 0)
@@ -969,8 +1051,8 @@
         0.0,
     ).astype(bf16)
     slots = lax.broadcasted_iota(jnp.int32, (cap, TOK), 0).astype(f32)
-    out_lane = lax.broadcasted_iota(jnp.int32, (2 * cap, 128), 1)
-    def groups(weights, x, dy, xs_now, ds_now, act_now, terms, ret_now):
+    out_lane = lax.broadcasted_iota(jnp.int32, (RING * cap, 128), 1)
+    def groups(weights, x, dy, xs_now, ds_now, act_now, places, terms, ret_now):
         def weight_loads():
             return [
                 pltpu.make_async_copy(w_own, weights.at[0], weight_sems.at[0]),
@@ -980,73 +1062,90 @@
         for copy in weight_loads():
             copy.start()
 
-        def loads(s):
-            copies = []
-            for g in range(2):
-                gx, gz = group_at(s, g)
-                copies.append(pltpu.make_async_copy(x_all.at[gx, gz], x.at[g], load_sems.at[g, 0]))
-                copies.append(pltpu.make_async_copy(dy_all.at[gx, gz], dy.at[g], load_sems.at[g, 1]))
-            return copies
+        def loads(s, g):
+            gx, gz = group_at(s, g)
+            return [
+                pltpu.make_async_copy(x_all.at[gx, gz], x.at[g % 2], load_sems.at[g % 2, 0]),
+                pltpu.make_async_copy(dy_all.at[gx, gz], dy.at[g % 2], load_sems.at[g % 2, 1]),
+            ]
 
         def rows_of(s):
-            start = s * 2 * cap
-            return pl.ds(start if isinstance(s, int) else pl.multiple_of(start, 2 * cap), 2 * cap)
+            start = s * RING * cap
+            if not isinstance(s, int):
+                start = pl.multiple_of(start, RING * cap)
+            return pl.ds(start, RING * cap)
 
         def row_stores(s):
-            at = rows_of(s)
             return [
-                pltpu.make_async_copy(xs_now, xs.at[:, at], store_sems.at[0]),
-                pltpu.make_async_copy(ds_now, ds.at[:, at], store_sems.at[1]),
+                pltpu.make_async_copy(xs_now, xs.at[:, rows_of(s)], store_sems.at[0]),
+                pltpu.make_async_copy(ds_now, ds.at[:, rows_of(s)], store_sems.at[1]),
             ]
 
         def act_store(s):
-            at = rows_of(s)
-            return pltpu.make_async_copy(act_now, act.at[:, at], store_sems.at[2])
+            return pltpu.make_async_copy(act_now, act.at[:, rows_of(s)], store_sems.at[2])
 
         def ret_store(s, g):
             gx, gz = group_at(s, g)
-            return pltpu.make_async_copy(ret_now.at[g], ret.at[gx, gz], store_sems.at[3 + g])
-
-        for copy in loads(0):
-            copy.start()
-
-        @pl.loop(0, 8)
+            dst = ret.at[gx, gz, :, :, pl.ds(0, width + 128)]
+            return pltpu.make_async_copy(ret_now.at[g % 2], dst, store_sems.at[3 + g % 2])
+
+        def ret_y_store(s, g):
+            gx, gz = group_at(s, g)
+            src = ret_now.at[g % 2, :, :, pl.ds(0, width)]
+            dst = ret.at[gx, gz, :, :, pl.ds(width + 128, width)]
+            return pltpu.make_async_copy(src, dst, store_sems.at[3 + g % 2])
+
+        def sums_at(s, point):
+            for k in range(RING):
+                if (k, point) in PLAN:
+                    pl.when(s == k)(functools.partial(act_at, (k, point)))
+
+        for g in range(2):
+            for copy in loads(0, g):
+                copy.start()
+
+        @pl.loop(0, RING)
         def _(s):
-            places, gates = [], []
-            for copy in loads(s):
-                copy.wait()
+            gates = []
 
             @pl.when(s > 0)
             def _():
                 for copy in row_stores(s):
                     copy.wait()
 
-            for g in range(2):
-                marks = x[g, :, :, width:].reshape(TOK, 128)
+            for g in range(RING):
+                for copy in loads(s, g):
+                    copy.wait()
+                marks = x[g % 2, :, :, width:].reshape(TOK, 128)
                 flags = dot(select, marks, NT)
                 slot = dot(flags.astype(bf16), before, NN)
                 place, gate = [], []
                 for j in range(locals_):
                     hit = (slots == slot[j : j + 1]) & (flags[j : j + 1] > 0.5)
                     place.append(jnp.where(hit, 1.0, 0.0))
-                    gate.append(
-                        jnp.sum(place[-1] * flags[locals_ + j : locals_ + j + 1], axis=1, keepdims=True)
-                    )
+                    chance = flags[locals_ + j : locals_ + j + 1]
+                    gate.append(jnp.sum(place[-1] * chance, axis=1, keepdims=True))
                 place = jnp.concatenate(place, axis=0).astype(bf16)
-                places.append(place)
+                places[g] = place
                 gates.append(gate)
-                picked = dot(place, x[g, :, :, :width].reshape(TOK, width), NN).astype(bf16)
-                picked_dy = dot(place, dy[g].reshape(TOK, width), NN).astype(bf16)
+                picked = dot(place, x[g % 2, :, :, :width].reshape(TOK, width), NN).astype(bf16)
                 for j in range(locals_):
                     xs_now[j, g * cap : (g + 1) * cap, :] = picked[j * cap : (j + 1) * cap]
-                    ds_now[j, g * cap : (g + 1) * cap, :] = picked_dy[j * cap : (j + 1) * cap]
+                picked = dot(place, dy[g % 2].reshape(TOK, width), NN).astype(bf16)
+                for j in range(locals_):
+                    ds_now[j, g * cap : (g + 1) * cap, :] = picked[j * cap : (j + 1) * cap]
+                if g < 2:
+                    for copy in loads(s, g + 2):
+                        copy.start()
+                else:
+
+                    @pl.when(s < RING - 1)
+                    def _():
+                        for copy in loads(s + 1, g - 2):
+                            copy.start()
+
             for copy in row_stores(s):
                 copy.start()
-
-            @pl.when(s < 7)
-            def _():
-                for copy in loads(s + 1):
-                    copy.start()
 
             @pl.when(s == 0)
             def _():
@@ -1057,17 +1156,14 @@
             def _():
                 act_store(s).wait()
                 for g in range(2):
-                    ret_store(s, g).wait()
-
-            for k in range(1, 8):
-                pl.when(s == k)(functools.partial(act_at, (k, 0)))
-
+                    ret_y_store(s, g).wait()
+
+            sums_at(s, 0)
             for j in range(locals_):
                 if j == half_experts:
-                    for k in range(1, 8):
-                        pl.when(s == k)(functools.partial(act_at, (k, 1)))
+                    sums_at(s, 1)
                 w = weights.at[j // half_experts, j % half_experts]
-                gate = jnp.concatenate([gates[g][j] for g in range(2)], axis=0)
+                gate = jnp.concatenate([gates[g][j] for g in range(RING)], axis=0)
                 up_in = dot(xs_now[j], w[0], NN)
                 up = dot(xs_now[j], w[1], NN)
                 d_raw = dot(ds_now[j], w[2], NN)
@@ -1075,33 +1171,47 @@
                 silu = up_in * sig
                 hidden = (silu * up).astype(bf16).astype(f32)
                 d_gate = jnp.sum(hidden * d_raw, axis=1, keepdims=True)
-                gated = (hidden * gate).astype(bf16)
                 d_hidden = d_raw * gate
-                d_up_in = (d_hidden * up * sig * (1.0 + up_in * (1.0 - sig))).astype(bf16)
-                d_up = (d_hidden * silu).astype(bf16)
-                act_now[j, :, :ff] = gated
-                act_now[j, :, ff : 2 * ff] = d_up_in
-                act_now[j, :, 2 * ff :] = d_up
-                y = dot(gated, w[2], NT).astype(bf16)
-                dx = (dot(d_up_in, w[0], NT) + dot(d_up, w[1], NT)).astype(bf16)
+                act_now[j, :, :ff] = (hidden * gate).astype(bf16)
+                act_now[j, :, ff : 2 * ff] = (
+                    d_hidden * up * sig * (1.0 + up_in * (1.0 - sig))
+                ).astype(bf16)
+                act_now[j, :, 2 * ff :] = (d_hidden * silu).astype(bf16)
                 dg = jnp.where(out_lane == ids[j], d_gate, 0.0).astype(bf16)
-                for g in range(2):
+                dx = dot(act_now[j, :, ff : 2 * ff], w[0], NT)
+                dx = (dx + dot(act_now[j, :, 2 * ff :], w[1], NT)).astype(bf16)
+                for g in range(RING):
                     part = slice(g * cap, (g + 1) * cap)
                     there = slice(j * cap, (j + 1) * cap)
-                    terms[g, there, :width] = y[part]
-                    terms[g, there, width : 2 * width] = dx[part]
-                    terms[g, there, 2 * width :] = dg[part]
+                    terms[g, there, :width] = dx[part]
+                    terms[g, there, width:] = dg[part]
             act_store(s).start()
-            for g in range(2):
-                for start, size in cuts:
-                    cut = slice(start, start + size)
-                    ret_now[g, :, :, cut] = (
-                        dot(places[g], terms[g, :, cut], TN).astype(bf16).reshape(RING, rows, size)
-                    )
+            for g in range(RING):
+                if g >= 2:
+                    ret_store(s, g - 2).wait()
+                ret_now[g % 2] = (
+                    dot(places[g], terms[g], TN).astype(bf16).reshape(RING, rows, width + 128)
+                )
                 ret_store(s, g).start()
+            for j in range(locals_):
+                if j == half_experts:
+                    for g in range(2):
+                        ret_store(s, g).wait()
+                    sums_at(s, 2)
+                w = weights.at[j // half_experts, j % half_experts]
+                y = dot(act_now[j, :, :ff], w[2], NT).astype(bf16)
+                for g in range(RING):
+                    terms[g, j * cap : (j + 1) * cap, :width] = y[g * cap : (g + 1) * cap]
+            for g in range(RING):
+                if g >= 2:
+                    ret_y_store(s, g - 2).wait()
+                ret_now[g % 2, :, :, :width] = (
+                    dot(places[g], terms[g, :, :width], TN).astype(bf16).reshape(RING, rows, width)
+                )
+                ret_y_store(s, g).start()
 
         for g in range(2):
-            ret_store(0, g).wait()
+            ret_y_store(0, g).wait()
         for copy in row_stores(0) + [act_store(0)]:
             copy.wait()
 
@@ -1111,11 +1221,12 @@
         pltpu.VMEM((2,) + w_own.shape, bf16),
         pltpu.VMEM((2, RING, rows, wide), bf16),
         pltpu.VMEM((2, RING, rows, width), bf16),
-        pltpu.VMEM((locals_, 2 * cap, width), bf16),
-        pltpu.VMEM((locals_, 2 * cap, width), bf16),
-        pltpu.VMEM((locals_, 2 * cap, 3 * ff), bf16),
-        pltpu.VMEM((2, locals_ * cap, ret.shape[4]), bf16),
-        pltpu.VMEM((2, RING, rows, ret.shape[4]), bf16),
+        pltpu.VMEM((locals_, RING * cap, width), bf16),
+        pltpu.VMEM((locals_, RING * cap, width), bf16),
+        pltpu.VMEM((locals_, RING * cap, 3 * ff), bf16),
+        pltpu.VMEM((RING, locals_ * cap, TOK), bf16),
+        pltpu.VMEM((RING, locals_ * cap, width + 128), bf16),
+        pltpu.VMEM((2, RING, rows, width + 128), bf16),
     )
 
     def ending(xs_e, ds_e, act_e, given, taken, summed):
@@ -1164,7 +1275,8 @@
                         cut = pl.ds(pl.multiple_of(q * (width // RING), width // RING), width // RING)
                         part = dot(rows_in[j % 2, :, cut], act_e[j % 2, :, cols_in], TN)
                         if own:
-                            summed[n % 2, cut, :] = part + taken[n % 2, cut, :].astype(f32)
+                            part = part + taken[n % 2, cut, :].astype(f32)
+                            summed[n % 2, cut, :] = part.astype(bf16)
                         else:
                             given[n, cut, :] = part.astype(bf16)
 
@@ -1177,10 +1289,10 @@
                     yield
 
         piece = work()
-        act_at((8, 0), piece)
-        go_on()
-        for _ in piece:
+        act_at((RING, 0), piece)
+        for _ in go_on():
             pass
+        run_all([piece])
         for n in (3 * half_experts - 2, 3 * half_experts - 1):
             store(n).wait()
         for k in sent:
@@ -1188,20 +1300,17 @@
         links.close()
 
     def go_on():
-        for p, (start, size) in enumerate(cuts):
-            acc = bufs[9 * p + 2]
-            home[:, start : start + size] = acc[3, links.at[orders[p][2]]]
+        bring_home()
         cot_load.wait()
-
         values = resid[...]
         inverse = lax.rsqrt(jnp.mean(values * values, axis=-1, keepdims=True) + EPSILON)
         hat = values * inverse
         moe_in = (hat * ffn_norm[...]).astype(bf16)
         probs, picks = chances[:, :EXPERTS], chances[:, EXPERTS:]
-        d_probs = home[:, 2 * width : 2 * width + EXPERTS].astype(f32) * picks
+        d_probs = home[:, width : width + EXPERTS].astype(f32) * picks
         d_logits = probs * (d_probs - jnp.sum(probs * d_probs, axis=-1, keepdims=True))
         d_logits = d_logits.astype(bf16)
-        d_moe = home[:, width : 2 * width].astype(f32) + dot(d_logits, router[...], NT)
+        d_moe = home[:, :width].astype(f32) + dot(d_logits, router[...], NN)
         d_hat = d_moe * ffn_norm[...]
         final = cot_now[...].astype(f32) + inverse * (
             d_hat - hat * jnp.mean(d_hat * hat, axis=-1, keepdims=True)
@@ -1219,11 +1328,15 @@
 
         sharing = gather_part(links, view, stage, (Y,))
         next(sharing)
-        out_mine[...] = (values + home[:, :width].astype(f32)).astype(bf16)
+        out_mine[...] = (values + home[:, width + 128 :].astype(f32)).astype(bf16)
         small_rows[:EXPERTS, :] = dot(d_logits, moe_in, TN)
         row = lax.broadcasted_iota(jnp.int32, (8, width), 0)
         d_ffn = jnp.sum(d_moe * hat, axis=0, keepdims=True)
         small_rows[EXPERTS:, :] = jnp.where(row == 1, d_ffn, 0.0)
+        yield
+        next(sharing)
+        next(sharing)
+        yield
         run_all([sharing])
         copy.wait()
 
@@ -1235,7 +1348,7 @@
         pltpu.VMEM((2,) + act.shape[1:], bf16),
         pltpu.VMEM((3 * half_experts, width, ff), bf16),
         pltpu.VMEM((2, width, ff), bf16),
-        pltpu.VMEM((2, width, ff), f32),
+        pltpu.VMEM((2, width, ff), bf16),
     )
 
 
@@ -1247,27 +1360,10 @@
     groups = RING * RING
     bf16, f32 = jnp.bfloat16, jnp.float32
     cols = 2 * width + 128
-    cuts = cut_as(9, 11, 13)
+    cuts = cut_as(*TILES)
     vmem, dma = pltpu.VMEM, pltpu.SemaphoreType.DMA
-    bufs, hbm_out = [], []
     shape = jax.ShapeDtypeStruct
-    for p, (_, size) in enumerate(cuts):
-        slots = 2 if p == 0 else 1
-        hbm_out += [
-            shape((2, 4, RING, rows // 2, size), bf16),
-            shape((2, 4, RING, rows, size), bf16),
-        ]
-        bufs += [
-            vmem((slots, 2, RING, rows // 2, size), bf16),
-            vmem((slots, 2, RING, rows // 2, size), bf16),
-            vmem((4, RING, rows, size), bf16),
-            vmem((2, RING, rows, size), bf16),
-            vmem((2, RING, rows // 2, size), bf16),
-            vmem((2, RING, rows, size), bf16),
-            vmem((2, rows // 2, size), bf16),
-            vmem((2, rows, size), bf16),
-            vmem((8, 128), bf16),
-        ]
+    hbm_out, bufs = ring_buffers(rows, cuts)
     in_vmem = pl.BlockSpec(memory_space=vmem)
     in_hbm = pl.BlockSpec(memory_space=pltpu.HBM)
     return pl.pallas_call(
@@ -1279,8 +1375,8 @@
             shape((rows, width), bf16),
             shape((rows, width), f32),
             shape((EXPERTS + 8, width), f32),
-            shape((locals_ // 2, 2, width, ff), f32),
-            shape((locals_ // 2, width, ff), f32),
+            shape((locals_ // 2, 2, width, ff), bf16),
+            shape((locals_ // 2, width, ff), bf16),
             shape((locals_, groups * CAP, width), bf16),
             shape((locals_, groups * CAP, width), bf16),
             shape((locals_, groups * CAP, 3 * ff), bf16),
@@ -1352,7 +1448,7 @@
 def back_kernel(
     lengths,
     d_resid,
-    weights,
+    all_weights,
     heads,
     raw,
     stats,
@@ -1390,14 +1486,29 @@
     rows_small,
     held,
     small_in,
+    whole,
+    row_sum,
+    row_out,
+    row_in,
+    row_in_x,
+    row_in_z,
+    row_in_pair,
     *rest,
 ):
     f32, bf16 = jnp.float32, jnp.bfloat16
-    bufs, (send_sems, recv_sems, local_sem) = rest[:-3], rest[-3:]
+    bufs, (weights, send_sems, recv_sems, local_sem, weight_sems) = rest[:-5], rest[-5:]
+    cols = q_gain.shape[1]
+
+    def weight_load(j):
+        cut = pl.ds(0, 3 * cols) if j else pl.ds(3 * cols, cols)
+        at = (slice(None),) * 4 + (cut,)
+        return pltpu.make_async_copy(all_weights.at[at], weights.at[at], weight_sems.at[j])
+
+    for j in range(2):
+        weight_load(j).start()
     links = Links((X, Z, Y), send_sems, recv_sems, pair=True, extra=[(Y, 2), (X, 2), (Z, 2)])
     x, z, y = links.at
     core = links.core
-    cols = q_gain.shape[1]
     rows, width = tokens.shape
     quarter = rows // RING
     block_rows = terms.shape[3]
@@ -1418,6 +1529,7 @@
     def weight(start, stop):
         return weights[:, :, :, :, start:stop].reshape(width, stop - start)
 
+    weight_load(0).wait()
     d_mixed[...] = dot(d_resid[...], weight(3 * cols, 4 * cols), NN).astype(bf16)
     rows_small[...] = jnp.zeros(rows_small.shape, f32)
     rows_small[: small_rows.shape[0], :] = small_rows[...]
@@ -1469,9 +1581,14 @@
         cut = pl.ds(start, size)
         return reduce_plane_part(links, order, functools.partial(region, cut), own[0], own[1:])
 
+    wide = 4 * cols
+    small_cols = rows_small.shape[0]
+    terms[:, :, :, :, wide:] = (
+        rows_small[...].T.astype(bf16).reshape(RING, RING, 2, block_rows, small_cols)
+    )
     fill(normed, d_proj[:, 2 * cols :], 2 * cols)
     fill(d_resid, mixed[...], 3 * cols)
-    first = reduction(0, 2 * cols, 2 * cols, (X, Z))
+    first = reduction(0, 2 * cols, 2 * cols + small_cols, (X, Z))
     next(first)
     total = end_sums(links, sent, sums, sums_in) / (HEADS * HEAD)
     for j in range(2):
@@ -1479,28 +1596,36 @@
         inverse = stats[:, j : j + 1]
         hat = raw[:, at] * inverse
         d_proj[:, at] = (inverse * (d_rot[:, at] - hat * total[:, j : j + 1])).astype(bf16)
+    fill(normed, d_proj[:, : 2 * cols], 0)
+    second = reduction(1, 0, 2 * cols, (Z, X))
+    next(second)
     next(first)
-    proj = weight(0, 3 * cols)
 
     def quarter_rows(step):
         return pl.ds(pl.multiple_of(links.rel(Y, step) * quarter, quarter), quarter)
 
+    weight_load(1).wait()
+    whole[...] = dot(d_proj[...], weight(0, 3 * cols), NT)
     for k, step in enumerate((2, 1, -1)):
-        parts[k] = dot(d_proj[quarter_rows(step), :], proj, NT).astype(bf16)
+        parts[k] = whole[quarter_rows(step), :].astype(bf16)
+    d_normed[...] = whole[mine, :]
     by_step = {2: parts.at[0], 1: parts.at[1], -1: parts.at[2]}
     summing = reduce_small(links, Y, by_step.get, d_normed, passing, landing)
     next(summing)
-    d_normed[...] = dot(d_proj[mine, :], proj, NT)
-    fill(normed, d_proj[:, : 2 * cols], 0)
-    second = reduction(1, 0, 2 * cols, (Z, X))
     next(second)
+    next(first)
     next(summing)
+    next(second)
     next(first)
     run_all([summing])
     hidden = tokens[mine, :].astype(f32)
     inverse = lax.rsqrt(jnp.mean(hidden * hidden, axis=-1, keepdims=True) + EPSILON)
     hat = hidden * inverse
-    rows_small[64:65, :] = jnp.sum(d_normed[...] * hat, axis=0, keepdims=True)
+    row_sum[...] = jnp.sum(d_normed[...] * hat, axis=0, keepdims=True)
+    row_out[3] = row_sum[...]
+    sent_row = [
+        links.send(row_out.at[3], row_in.at[k], links.peer(Y, k + 1)) for k in range(3)
+    ]
     d_hat = d_normed[...] * attn_norm[...]
     final = d_resid_mine[...] + inverse * (
         d_hat - hat * jnp.mean(d_hat * hat, axis=-1, keepdims=True)
@@ -1515,23 +1640,27 @@
     sharing = gather_part(links, grads_view, grads_in.at[y], (Y,))
     next(sharing)
     next(out_sharing)
-    wide = 4 * cols
-    terms[:, :, :, :, wide:] = (
-        rows_small[...].T.astype(bf16).reshape(RING, RING, 2, block_rows, rows_small.shape[0])
-    )
-    third = reduction(2, wide, rows_small.shape[0], (X, Z))
-    next(third)
+
+    def row_add(sent, landed):
+        for k in range(3):
+            links.arrive(sent[k], landed.at[k])
+        row_sum[...] = row_sum[...] + landed[0] + landed[1] + landed[2]
+
+    def row_on(axis, landed):
+        row_out[axis] = row_sum[...]
+        return [
+            links.send(row_out.at[axis], landed.at[k], links.peer(axis, step))
+            for k, step in enumerate((2, 1, -1))
+        ]
+
+    run_all([first])
+    here = terms.at[x, z, core]
+    small = here.at[:, pl.ds(wide, small_cols)]
+    sent = [links.send(small, small_in.at[k], links.peer(Y, k + 1)) for k in range(3)]
+    row_add(sent_row, row_in)
+    sent_row = row_on(X, row_in_x)
     next(second)
-    next(first, None)
-    next(second, None)
-    run_all([third, first, second, sharing, out_sharing])
-
-    here = terms.at[x, z, core]
-    small = here.at[:, pl.ds(wide, rows_small.shape[0])]
-    sent = [links.send(small, small_in.at[k], links.peer(Y, k + 1)) for k in range(3)]
-    for j in range(3):
-        grad_qkv[j] = here[:, j * cols : (j + 1) * cols].astype(f32)
-    grad_out[...] = here[:, 3 * cols : 4 * cols].astype(f32)
+    next(sharing)
     total = small[...].astype(f32)
     for k in range(3):
         links.arrive(sent[k], small_in.at[k])
@@ -1539,21 +1668,34 @@
     held[x, z, core] = total.astype(bf16)
     own = held.at[x, z, core]
     sent = [links.send(own, own, links.peer(X, step)) for step in (2, 1, -1)]
-    for q in range(RING):
-        input_grad[q * quarter : (q + 1) * quarter, :] = grads_in[q].astype(f32)
+    grad_out[...] = here[:, 3 * cols : 4 * cols].astype(f32)
+    grad_qkv[2] = here[:, 2 * cols : 3 * cols].astype(f32)
+    row_add(sent_row, row_in_x)
+    sent_row = row_on(Z, row_in_z)
     for k, step in zip(sent, (2, 1, -1)):
         links.arrive(k, held.at[links.rel(X, -step), z, core])
     own = held.at[:, z, core]
     sent = [links.send(own, own, links.peer(Z, step)) for step in (2, 1, -1)]
+    next(second, None)
+    next(sharing)
+    next(out_sharing)
+    row_add(sent_row, row_in_z)
+    row_out[Y] = row_sum[...]
+    sent_row = links.send(row_out.at[Y], row_in_pair, links.pair())
     for k, step in zip(sent, (2, 1, -1)):
         links.arrive(k, held.at[:, links.rel(Z, -step), core])
     own = held.at[:, :, core]
     k = links.send(own, own, links.pair())
+    run_all([second, sharing, out_sharing])
+    for j in range(2):
+        grad_qkv[j] = here[:, j * cols : (j + 1) * cols].astype(f32)
+    for q in range(RING):
+        input_grad[q * quarter : (q + 1) * quarter, :] = grads_in[q]
     links.arrive(k, held.at[:, :, 1 - core])
-    total = held[...].astype(f32).reshape(width, rows_small.shape[0])
-    grad_router[...] = total[:, :EXPERTS]
-    rows_small[...] = total.T
-    grad_attn[...] = rows_small[64:65, :]
+    rows_small[...] = held[...].astype(f32).reshape(width, small_cols).T
+    grad_router[...] = rows_small[:EXPERTS, :]
+    links.arrive(sent_row, row_in_pair)
+    grad_attn[...] = row_sum[...] + row_in_pair[...]
     grad_ffn[...] = rows_small[65:66, :]
     out_here.wait()
     cut = pl.ds(pl.multiple_of(y * cols, cols), cols)
@@ -1591,20 +1733,21 @@
     freqs = jnp.concatenate([freqs, freqs])[None, :]
     in_vmem = pl.BlockSpec(memory_space=pltpu.VMEM)
     shape = jax.ShapeDtypeStruct
+    in_hbm = pl.BlockSpec(memory_space=pltpu.HBM)
     vmem = pltpu.VMEM
     buffers = []
-    for size in (2 * cols, 2 * cols, 128):
+    for size in (2 * cols + 128, 2 * cols):
         buffers += plane_buffers(block_rows, size)
     return pl.pallas_call(
         back_kernel,
-        in_specs=[pl.BlockSpec(memory_space=pltpu.SMEM)] + [in_vmem] * 16,
-        out_specs=[in_vmem, pl.BlockSpec(memory_space=pltpu.HBM)] + [in_vmem] * 7,
+        in_specs=[pl.BlockSpec(memory_space=pltpu.SMEM), in_vmem, in_hbm] + [in_vmem] * 14,
+        out_specs=[in_vmem, in_hbm] + [in_vmem] * 7,
         out_shape=[
-            shape((rows, width), f32),
+            shape((rows, width), bf16),
             shape((rows, width), bf16),
             shape((3, block_rows, cols), f32),
             shape((block_rows, cols), f32),
-            shape((width, EXPERTS), f32),
+            shape((EXPERTS, width), f32),
             shape((1, width), f32),
             shape((1, width), f32),
             shape((1, cols), f32),
@@ -1625,12 +1768,21 @@
             vmem((128, width), f32),
             vmem((RING, RING, 2, block_rows, 128), bf16),
             vmem((3, block_rows, 128), bf16),
+            vmem((rows, width), f32),
+            vmem((1, width), f32),
+            vmem((4, 1, width), f32),
+            vmem((3, 1, width), f32),
+            vmem((3, 1, width), f32),
+            vmem((3, 1, width), f32),
+            vmem((1, width), f32),
         ]
         + buffers
         + [
+            vmem(weights.shape, bf16),
             pltpu.SemaphoreType.DMA((80,)),
             pltpu.SemaphoreType.DMA((80,)),
             pltpu.SemaphoreType.DMA,
+            pltpu.SemaphoreType.DMA((2,)),
         ],
         compiler_params=pltpu.CompilerParams(
             collective_id=collective_id, has_side_effects=True, vmem_limit_bytes=VMEM_LIMIT
@@ -1672,19 +1824,19 @@
     expert_ids,
     cotangent,
 ):
-    blocks = jnp.concatenate([qkv_weights[0], qkv_weights[1], qkv_weights[2], out_weight], axis=1)
     pairs = [(i, i ^ 1) for i in range(lax.axis_size("expert"))]
     pair_weights = lax.ppermute(expert_weights, "expert", pairs)
     all_weights, rows_all, cot_rows, normed_b, heads, raw, inverses, lse, mixed_b, resid, chances = front(
         lengths,
-        blocks,
+        qkv_weights,
+        out_weight,
         tokens,
         attn_norm[None],
         q_gain[None],
         k_gain[None],
         ffn_norm[None],
-        router,
-        expert_ids,
+        router.T,
+        expert_ids.T,
         cotangent,
         1,
     )
@@ -1695,7 +1847,7 @@
         pair_weights,
         resid,
         chances,
-        router,
+        router.T,
         ffn_norm[None],
         cotangent,
         3,
@@ -1721,16 +1873,16 @@
     )
     return (
         output,
-        input_grad,
+        input_grad.astype(jnp.float32),
         grad_attn[0],
         grad_qkv,
         grad_out,
         grad_q[0],
         grad_k[0],
         grad_ffn[0],
-        grad_router,
-        grad_experts,
-        grad_down,
+        grad_router.T,
+        grad_experts.astype(jnp.float32),
+        grad_down.astype(jnp.float32),
     )
 
 

time: 507 us -> 470 us (0.927)
  the two profiles are of different devices: /device:TPU:1 before, /device:TPU:0 now
where the time goes in v2:
time: 470 us; the launch traced here: 462 us
  Pallas kernels  445 us (95%)
  other arithmetic  10 us (2%)
  local copies, waits for them, and re-layouts  5.56 us (1%)
    pallas_call x1, Pallas kernels, experts(): pl.pallas_call(functools.partial(experts_kernel, cuts), in_specs=[in_hbm]...  195 us
    pallas_call x1, Pallas kernels, front(): pl.pallas_call(functools.partial(front_kernel, cut_as(4, 6, 7), cut_as(4,...  179 us
    pallas_call x1, Pallas kernels, back(): pl.pallas_call(back_kernel, in_specs=[pl.BlockSpec(memory_space=pltpu.SME...  71.5 us
  transfers between devices with their start and end apart: 1, of which 0 were waited for; matrix products, arithmetic and copies ran while one was open for 0% of the time, Pallas kernels for 39%

profile of v2, /device:TPU:0, one launch (start us, length us, event | category | flops | bytes accessed | tf_op | source)
XLA Modules:
  0.0 462.1 jit_solution(12393492927736119677)
XLA Ops:
  0.6 0.1 collective-permute-start
  0.8 0.6 maximum_bitcast_fusion.freqs
  1.3 178.9 %front.1 = (bf16[4,4,2,64,2048]{4,3,2,1,0:T(8,128)(2,1)}, bf16[4,4,4,64,2176]{4,3,2,1,0:T(8,128)(2,1)}, bf16[4,4,4,64,2048]{4,3,2,1,0:T(8,128)(2,1)}, bf16[256,2...) custom-call(s32[1,4]{1,0:T(1,128)} %lengths.3, ...), custom_call_target="tpu_custom_call" | custom-call | tf_op jit(solution)/shard_map/front/pallas_call | solution.py:553
  180.3 0.0 collective-permute-done.w_pair
  180.3 194.9 %experts.1 = (bf16[256,2048]{1,0:T(8,128)(2,1)}, bf16[64,2048]{1,0:T(8,128)(2,1)}, f32[64,2048]{1,0:T(8,128)}, f32[72,2048]{1,0:T(8,128)}, bf16[2,2,2048,256]{3,...) custom-call(bf16[4,4,4,64,2176]{4,3,2,1,0:T(8,128)(2,1)} %get-tuple-, ...), custom_call_target="tpu_custom_call" | custom-call | tf_op jit(solution)/shard_map/experts/pallas_call | solution.py:1369
  375.1 0.0 copy-start.1
  375.1 71.5 %back.1 = (bf16[256,2048]{1,0:T(8,128)(2,1)}, bf16[256,2048]{1,0:T(8,128)(2,1)}, f32[3,64,512]{2,1,0:T(8,128)}, f32[64,512]{1,0:T(8,128)}, f32[64,2048]{1,0:T(8,...) custom-call(s32[1,4]{1,0:T(1,128)} %lengths.3, ...), custom_call_target="tpu_custom_call" | custom-call | tf_op jit(solution)/shard_map/back/pallas_call | solution.py:1741
  446.6 0.0 copy-start
  446.6 2.9 convert_element_type.9
  449.6 0.0 copy-done.1
  449.6 2.3 convert_element_type.11
  452.0 4.1 convert_element_type.10
  456.1 0.0 copy-done.2
  456.1 1.0 copy.31
  457.1 0.0 copy-done.7
  457.1 0.6 copy.32
  457.7 0.7 copy.33
  458.5 0.7 copy.34
  459.1 0.0 copy-done.9
  459.1 0.6 copy.35
  459.7 0.6 copy.36
  460.3 0.6 copy.37
  460.9 0.0 copy-done.3
  460.9 0.8 copy.38
  (14 shorter events, 0.0 us)
Async XLA Ops:
  0.6 179.6 %collective-permute-start = (bf16[2,3,2048,256]{3,2,1,0:T(8,128)(2,1)}, bf16[2,3,2048,256]{3,2,1,0:T(8,128)(2,1)}, u32[]{:S(2)}, u32[]{:S(2)}) collective-permute-start(bf16[2,3,2048,256]{3,2,1,0:T(8,128)(2,1)} %w_own.1), channel_id=1, source_target_pairs={{0,4},{4,0},{8,12},{12,8},{16,20},{20,16},{24,28},{28,24},{1,5},{5... | collective-permute-start | bytes 18874376 | tf_op jit(solution)/shard_map/ppermute | solution.py:1828
  375.1 74.5 %copy-start.1 = (bf16[2,2048,256]{2,1,0:T(8,128)(2,1)S(1)}, bf16[2,2048,256]{2,1,0:T(8,128)(2,1)}, u32[]{:S(2)}) copy-start(bf16[2,2048,256]{2,1,0:T(8,128)(2,1)} %get-tuple-element.62) | copy-start | bytes 6291460
  446.6 5.3 %copy-start = (bf16[2,2,2048,256]{3,2,1,0:T(8,128)(2,1)S(1)}, bf16[2,2,2048,256]{3,2,1,0:T(8,128)(2,1)}, u32[]{:S(2)}) copy-start(bf16[2,2,2048,256]{3,2,1,0:T(8,128)(2,1)} %get-tuple-element.61) | copy-start | bytes 12582916
  451.9 4.2 copy-start.2
  451.9 5.2 %copy-start.7 = (f32[1,2048]{1,0:T(1,128)S(1)}, f32[1,2048]{1,0:T(1,128)}, u32[]{:S(2)}) copy-start(f32[1,2048]{1,0:T(1,128)} %get-tuple-element.54) | copy-start | bytes 24580
  451.9 5.8 %copy-start.4 = (f32[3,64,512]{2,1,0:T(8,128)S(1)}, f32[3,64,512]{2,1,0:T(8,128)}, u32[]{:S(2)}) copy-start(f32[3,64,512]{2,1,0:T(8,128)} %get-tuple-element.77) | copy-start | bytes 1179652
  451.9 6.5 %copy-start.5 = (f32[64,512]{1,0:T(8,128)S(1)}, f32[64,512]{1,0:T(8,128)}, u32[]{:S(2)}) copy-start(f32[64,512]{1,0:T(8,128)} %get-tuple-element.78) | copy-start | bytes 393220
  452.0 7.2 %copy-start.9 = (f32[1,512]{1,0:T(1,128)S(1)}, f32[1,512]{1,0:T(1,128)}, u32[]{:S(2)}) copy-start(f32[1,512]{1,0:T(1,128)} %get-tuple-element.57) | copy-start | bytes 6148
  452.0 7.7 %copy-start.8 = (f32[1,512]{1,0:T(1,128)S(1)}, f32[1,512]{1,0:T(1,128)}, u32[]{:S(2)}) copy-start(f32[1,512]{1,0:T(1,128)} %get-tuple-element.58) | copy-start | bytes 6148
  452.0 8.3 %copy-start.6 = (f32[1,2048]{1,0:T(1,128)S(1)}, f32[1,2048]{1,0:T(1,128)}, u32[]{:S(2)}) copy-start(f32[1,2048]{1,0:T(1,128)} %get-tuple-element.59) | copy-start | bytes 24580
  452.0 8.9 %copy-start.3 = (f32[64,2048]{1,0:T(8,128)S(1)}, f32[64,2048]{1,0:T(8,128)}, u32[]{:S(2)}) copy-start(f32[64,2048]{1,0:T(8,128)} %get-tuple-element.60) | copy-start | bytes 1572868
